TPU v7x, 32 devices: a whole 2x2x4 slice. The times are simulated.
32 devices in a mesh: ctx: 16 (over z, y, core), fsdp: 2 (over x).
Axes of the slice: x: 2, y: 2, z: 4, core: 2. Of those that a mesh axis runs over, the one named last changes fastest.
Arguments:
- tokens: bfloat16 [2, 2048, 960], P('fsdp', 'ctx'), may hold values from -6 to 6
- pair_of: int32 [2, 16], P('fsdp'), may hold values from 0 to 15, each once within a row
- attn_gain: bfloat16 [960], P('fsdp'), may hold values from 0.25 to 1.75
- w_query: bfloat16 [960, 960], P('fsdp'), may hold values from -0.1875 to 0.1875
- w_key: bfloat16 [960, 320], P('fsdp'), may hold values from -0.1875 to 0.1875
- w_value: bfloat16 [960, 320], P('fsdp'), may hold values from -0.1875 to 0.1875
- w_out: bfloat16 [960, 960], P('fsdp'), may hold values from -0.75 to 0.75
- ffn_gain: bfloat16 [960], P('fsdp'), may hold values from 0.25 to 1.75
- w_gate: bfloat16 [960, 2560], P('fsdp'), may hold values from -0.1875 to 0.1875
- w_up: bfloat16 [960, 2560], P('fsdp'), may hold values from -0.1875 to 0.1875
- w_down: bfloat16 [2560, 960], P('fsdp'), may hold values from -0.125 to 0.125
- out_grad: bfloat16 [2, 2048, 960], P('fsdp', 'ctx'), may hold values from -6 to 6
Outputs:
- block_out: bfloat16 [2, 2048, 960], P('fsdp', 'ctx')
- grad_in: float32 [2, 2048, 960], P('fsdp', 'ctx')
- grad_attn_gain: float32 [960], P('fsdp')
- grad_query: float32 [960, 960], P('fsdp')
- grad_key: float32 [960, 320], P('fsdp')
- grad_value: float32 [960, 320], P('fsdp')
- grad_out_proj: float32 [960, 960], P('fsdp')
- grad_ffn_gain: float32 [960], P('fsdp')
- grad_gate: float32 [960, 2560], P('fsdp')
- grad_up: float32 [960, 2560], P('fsdp')
- grad_down: float32 [2560, 960], P('fsdp')
Inputs may be any that keep to these rules, and one draw needn't show every extreme that they name: `pair_of`: each row names every number below 16 once.
All inputs are finite; a program needn't handle non-finite values.
Results may differ from a plain program's by a relative error of at most 0.024.
Values may be sent and summed in bfloat16 or wider, within the bound.
A program may use at most 192 MiB of HBM per device.

v0:
```python
import math

import jax
import jax.numpy as jnp
from jax import lax
from jax.sharding import PartitionSpec as P

HEADS = 15
KV_HEADS = 5
HEAD = 64


NORM_EPS = 1e-05
ROPE_BASE = 100000.0
MASKED = -1e30
TILE_KEYS = 512


def matmul(left_mat, right_mat):
    return jnp.dot(left_mat, right_mat, preferred_element_type=jnp.float32)


def contract_rows(left_mat, right_mat):
    return lax.dot_general(
        left_mat, right_mat, (((0,), (0,)), ((), ())), preferred_element_type=jnp.float32
    )


def contract_cols(left_mat, right_mat):
    return lax.dot_general(
        left_mat, right_mat, (((1,), (1,)), ((), ())), preferred_element_type=jnp.float32
    )


def rope_tables(positions, head_size):
    half_size = head_size // 2
    exponent = jnp.arange(half_size, dtype=jnp.float32) * (2.0 / head_size)
    frequency = jnp.exp(-exponent * math.log(ROPE_BASE))
    angle_table = positions.astype(jnp.float32)[:, None] * frequency[None, :]
    return (jnp.cos(angle_table)[:, None, :], jnp.sin(angle_table)[:, None, :])


def rotate(vectors, cosine_table, sine_table):
    half_size = vectors.shape[-1] // 2
    front_half = vectors[..., :half_size]
    back_half = vectors[..., half_size:]
    return jnp.concatenate(
        [
            front_half * cosine_table - back_half * sine_table,
            back_half * cosine_table + front_half * sine_table,
        ],
        axis=-1,
    )


def unrotate(grad_vec, cosine_table, sine_table):
    half_size = grad_vec.shape[-1] // 2
    front_half = grad_vec[..., :half_size]
    back_half = grad_vec[..., half_size:]
    return jnp.concatenate(
        [
            front_half * cosine_table + back_half * sine_table,
            back_half * cosine_table - front_half * sine_table,
        ],
        axis=-1,
    )


def inverse_rms(source):
    return lax.rsqrt(jnp.mean(source * source, axis=-1, keepdims=True) + NORM_EPS)


def norm_back(grad_normed, source, inverse, gain_vec):
    scaled = grad_normed * gain_vec
    inner = jnp.sum(scaled * source, axis=-1, keepdims=True) / source.shape[-1]
    grad_source = inverse * scaled - source * (inverse * inverse * inverse) * inner
    grad_gain = jnp.sum(grad_normed * source * inverse, axis=0)
    return (grad_source, grad_gain)


def reorder_blocks(rows_in, block_order, block_rows):
    blocks = rows_in.reshape((block_order.shape[0], block_rows) + rows_in.shape[1:])
    return jnp.take(blocks, block_order, axis=0).reshape(rows_in.shape)


def tile_scores(queries, key_tile, query_pos, first_key, score_scale):
    key_span = key_tile.shape[0]
    scores = (
        jnp.einsum("qkgd,tkd->kgqt", queries, key_tile, preferred_element_type=jnp.float32)
        * score_scale
    )
    key_pos = first_key + jnp.arange(key_span, dtype=jnp.int32)
    visible = key_pos[None, None, None, :] <= query_pos[None, None, :, None]
    return jnp.where(visible, scores, MASKED)


def block_forward(
    queries, query_pos, keys_natural, values_natural, tile_count, key_span, score_scale
):
    stat_shape = (queries.shape[1], queries.shape[2], queries.shape[0])

    def stats_step(tile_index, running):
        row_max, row_sum = running
        key_tile = lax.dynamic_slice_in_dim(keys_natural, tile_index * key_span, key_span, 0)
        scores = tile_scores(queries, key_tile, query_pos, tile_index * key_span, score_scale)
        new_max = jnp.maximum(row_max, jnp.max(scores, axis=-1))
        row_sum = row_sum * jnp.exp(row_max - new_max) + jnp.sum(
            jnp.exp(scores - new_max[..., None]), axis=-1
        )
        return (new_max, row_sum)

    initial = (jnp.full(stat_shape, MASKED, jnp.float32), jnp.zeros(stat_shape, jnp.float32))
    row_max, row_sum = lax.fori_loop(0, tile_count, stats_step, initial)

    def value_step(tile_index, accumulated):
        key_tile = lax.dynamic_slice_in_dim(keys_natural, tile_index * key_span, key_span, 0)
        value_tile = lax.dynamic_slice_in_dim(values_natural, tile_index * key_span, key_span, 0)
        scores = tile_scores(queries, key_tile, query_pos, tile_index * key_span, score_scale)
        weights = (jnp.exp(scores - row_max[..., None]) / row_sum[..., None]).astype(jnp.bfloat16)
        return accumulated + jnp.einsum(
            "kgqt,tkd->qkgd", weights, value_tile, preferred_element_type=jnp.float32
        )

    mixed_part = lax.fori_loop(0, tile_count, value_step, jnp.zeros(queries.shape, jnp.float32))
    return (mixed_part, row_max, row_sum)


def block_backward(
    queries,
    query_pos,
    keys_natural,
    values_natural,
    tile_count,
    key_span,
    score_scale,
    row_max,
    row_sum,
    grad_mixed,
    row_delta,
    grad_keys,
    grad_values,
):

    def grad_step(tile_index, running):
        grad_query, key_buffer, value_buffer = running
        first_key = tile_index * key_span
        key_tile = lax.dynamic_slice_in_dim(keys_natural, first_key, key_span, 0)
        value_tile = lax.dynamic_slice_in_dim(values_natural, first_key, key_span, 0)
        scores = tile_scores(queries, key_tile, query_pos, first_key, score_scale)
        probs = jnp.exp(scores - row_max[..., None]) / row_sum[..., None]
        probs_low = probs.astype(jnp.bfloat16)
        grad_probs = jnp.einsum(
            "qkgd,tkd->kgqt", grad_mixed, value_tile, preferred_element_type=jnp.float32
        )
        grad_scores = (probs * (grad_probs - row_delta[..., None])).astype(jnp.bfloat16)
        grad_query = grad_query + jnp.einsum(
            "kgqt,tkd->qkgd", grad_scores, key_tile, preferred_element_type=jnp.float32
        )
        key_part = jnp.einsum(
            "kgqt,qkgd->tkd", grad_scores, queries, preferred_element_type=jnp.float32
        )
        value_part = jnp.einsum(
            "kgqt,qkgd->tkd", probs_low, grad_mixed, preferred_element_type=jnp.float32
        )
        key_buffer = lax.dynamic_update_slice_in_dim(
            key_buffer,
            lax.dynamic_slice_in_dim(key_buffer, first_key, key_span, 0) + key_part,
            first_key,
            0,
        )
        value_buffer = lax.dynamic_update_slice_in_dim(
            value_buffer,
            lax.dynamic_slice_in_dim(value_buffer, first_key, key_span, 0) + value_part,
            first_key,
            0,
        )
        return (grad_query, key_buffer, value_buffer)

    initial = (jnp.zeros(queries.shape, jnp.float32), grad_keys, grad_values)
    return lax.fori_loop(0, tile_count, grad_step, initial)


def body(
    tokens,
    pair_of,
    attn_gain,
    w_query,
    w_key,
    w_value,
    w_out,
    ffn_gain,
    w_gate,
    w_up,
    w_down,
    out_grad,
):
    inputs = tokens[0].astype(jnp.float32)
    local_rows = inputs.shape[0]
    half_rows = local_rows // 2
    pair_row = pair_of[0]
    pair_total = lax.axis_size("ctx")
    seq_length = pair_total * local_rows
    key_span = min(TILE_KEYS, seq_length)
    score_scale = HEAD ** (-0.5)
    group_size = HEADS // KV_HEADS
    query_full, key_full, value_full, out_full, gain_attn, gain_ffn = (
        lax.all_gather(w_query, "fsdp", axis=0, tiled=True),
        lax.all_gather(w_key, "fsdp", axis=0, tiled=True),
        lax.all_gather(w_value, "fsdp", axis=0, tiled=True),
        lax.all_gather(w_out, "fsdp", axis=0, tiled=True),
        lax.all_gather(attn_gain, "fsdp", axis=0, tiled=True),
        lax.all_gather(ffn_gain, "fsdp", axis=0, tiled=True),
    )
    gain_attn = gain_attn.astype(jnp.float32)
    gain_ffn = gain_ffn.astype(jnp.float32)
    slot_ids = jnp.arange(pair_total, dtype=jnp.int32)
    own_pair = jnp.sum(jnp.where(slot_ids == lax.axis_index("ctx"), pair_row, 0))
    own_blocks = jnp.stack([own_pair, 2 * pair_total - 1 - own_pair])
    offsets = jnp.arange(half_rows, dtype=jnp.int32)
    own_pos = (own_blocks[:, None] * half_rows + offsets[None, :]).reshape(local_rows)
    cosine_table, sine_table = rope_tables(own_pos, HEAD)
    holder = jnp.sum(
        jnp.where(pair_row[None, :] == slot_ids[:, None], slot_ids[None, :], 0), axis=1
    )
    natural_order = jnp.concatenate([holder * 2, (holder * 2 + 1)[::-1]])
    device_order = jnp.stack([pair_row, 2 * pair_total - 1 - pair_row], axis=1).reshape(
        2 * pair_total
    )
    inverse_one = inverse_rms(inputs)
    normed_one = (inputs * inverse_one * gain_attn).astype(jnp.bfloat16)
    query_raw = matmul(normed_one, query_full).reshape(local_rows, HEADS, HEAD)
    key_raw = matmul(normed_one, key_full).reshape(local_rows, KV_HEADS, HEAD)
    value_local = matmul(normed_one, value_full).astype(jnp.bfloat16)
    queries = (
        rotate(query_raw, cosine_table, sine_table)
        .astype(jnp.bfloat16)
        .reshape(local_rows, KV_HEADS, group_size, HEAD)
    )
    key_local = (
        rotate(key_raw, cosine_table, sine_table)
        .astype(jnp.bfloat16)
        .reshape(local_rows, KV_HEADS * HEAD)
    )
    key_device, value_device = (
        lax.all_gather(key_local, "ctx", axis=0, tiled=True),
        lax.all_gather(value_local, "ctx", axis=0, tiled=True),
    )
    keys_natural = reorder_blocks(key_device, natural_order, half_rows).reshape(
        seq_length, KV_HEADS, HEAD
    )
    values_natural = reorder_blocks(value_device, natural_order, half_rows).reshape(
        seq_length, KV_HEADS, HEAD
    )
    tile_counts = (own_blocks * half_rows + half_rows - 1) // key_span + 1
    mixed_parts = []
    stat_parts = []
    for half_index in range(2):
        low_row = half_index * half_rows
        high_row = low_row + half_rows
        mixed_part, row_max, row_sum = block_forward(
            queries[low_row:high_row],
            own_pos[low_row:high_row],
            keys_natural,
            values_natural,
            tile_counts[half_index],
            key_span,
            score_scale,
        )
        mixed_parts.append(mixed_part)
        stat_parts.append((row_max, row_sum))
    mixed_full = jnp.concatenate(mixed_parts, axis=0)
    mixed_low = mixed_full.reshape(local_rows, HEADS * HEAD).astype(jnp.bfloat16)
    residual = inputs + matmul(mixed_low, out_full)
    inverse_two = inverse_rms(residual)
    normed_two = (residual * inverse_two * gain_ffn).astype(jnp.bfloat16)
    pieces = (
        lax.all_gather(w_gate, "fsdp", axis=0, tiled=True),
        lax.all_gather(w_up, "fsdp", axis=0, tiled=True),
    )
    columns = normed_two
    gate_pre = matmul(columns, pieces[0])
    up_pre = matmul(columns, pieces[1])
    sigmoid_gate = jax.nn.sigmoid(gate_pre)
    activated = gate_pre * sigmoid_gate
    hidden = (activated * up_pre).astype(jnp.bfloat16)
    columns = hidden
    down_out = matmul(columns, lax.all_gather(w_down, "fsdp", axis=0, tiled=True))
    block_out = (residual + down_out).astype(jnp.bfloat16)[None]
    grad_z = out_grad[0]
    grad_hidden = contract_cols(grad_z, lax.all_gather(w_down, "fsdp", axis=0, tiled=True))
    grad_gate_low = (
        grad_hidden * up_pre * sigmoid_gate * (1.0 + gate_pre * (1.0 - sigmoid_gate))
    ).astype(jnp.bfloat16)
    grad_up_low = (grad_hidden * activated).astype(jnp.bfloat16)
    pieces = (
        lax.all_gather(w_gate, "fsdp", axis=0, tiled=True),
        lax.all_gather(w_up, "fsdp", axis=0, tiled=True),
    )
    part = contract_cols(grad_gate_low, pieces[0]) + contract_cols(grad_up_low, pieces[1])
    grad_both = jnp.concatenate([grad_gate_low, grad_up_low], axis=1)
    grad_resid, grad_ffn_gain_term = norm_back(part, residual, inverse_two, gain_ffn)
    grad_resid = grad_resid + grad_z.astype(jnp.float32)
    grad_attn_low = grad_resid.astype(jnp.bfloat16)
    grad_mixed = (
        contract_cols(grad_attn_low, out_full)
        .astype(jnp.bfloat16)
        .reshape(local_rows, KV_HEADS, group_size, HEAD)
    )
    delta_all = jnp.moveaxis(jnp.sum(grad_mixed.astype(jnp.float32) * mixed_full, axis=-1), 0, -1)
    zero_keys = jnp.zeros((seq_length, KV_HEADS, HEAD), jnp.float32)
    grad_keys_nat, grad_values_nat = (zero_keys, zero_keys)
    query_grads = []
    for half_index in range(2):
        low_row = half_index * half_rows
        high_row = low_row + half_rows
        grad_query_part, grad_keys_nat, grad_values_nat = block_backward(
            queries[low_row:high_row],
            own_pos[low_row:high_row],
            keys_natural,
            values_natural,
            tile_counts[half_index],
            key_span,
            score_scale,
            stat_parts[half_index][0],
            stat_parts[half_index][1],
            grad_mixed[low_row:high_row],
            delta_all[..., low_row:high_row],
            grad_keys_nat,
            grad_values_nat,
        )
        query_grads.append(grad_query_part)
    grad_query_rot = (jnp.concatenate(query_grads, axis=0) * score_scale).reshape(
        local_rows, HEADS, HEAD
    )
    grad_query_low = (
        unrotate(grad_query_rot, cosine_table, sine_table)
        .astype(jnp.bfloat16)
        .reshape(local_rows, HEADS * HEAD)
    )
    grad_key_dev = reorder_blocks(
        (grad_keys_nat * score_scale).reshape(seq_length, KV_HEADS * HEAD), device_order, half_rows
    )
    grad_value_dev = reorder_blocks(
        grad_values_nat.reshape(seq_length, KV_HEADS * HEAD), device_order, half_rows
    )
    key_sum, value_sum = (
        lax.psum_scatter(
            grad_key_dev.astype(jnp.bfloat16), "ctx", scatter_dimension=0, tiled=True
        ).astype(jnp.float32),
        lax.psum_scatter(
            grad_value_dev.astype(jnp.bfloat16), "ctx", scatter_dimension=0, tiled=True
        ).astype(jnp.float32),
    )
    grad_key_low = (
        unrotate(key_sum.reshape(local_rows, KV_HEADS, HEAD), cosine_table, sine_table)
        .astype(jnp.bfloat16)
        .reshape(local_rows, KV_HEADS * HEAD)
    )
    grad_value_low = value_sum.astype(jnp.bfloat16)
    grad_normed_one = (
        contract_cols(grad_query_low, query_full)
        + contract_cols(grad_key_low, key_full)
        + contract_cols(grad_value_low, value_full)
    )
    grad_inputs, grad_attn_gain_term = norm_back(grad_normed_one, inputs, inverse_one, gain_attn)
    grad_in = (grad_resid + grad_inputs)[None]
    ff_cols = w_gate.shape[1]
    down_part = lax.psum_scatter(
        contract_rows(hidden, grad_z).astype(jnp.bfloat16), "fsdp", scatter_dimension=0, tiled=True
    )
    gate_up_part = lax.psum_scatter(
        contract_rows(normed_two, grad_both).astype(jnp.bfloat16),
        "fsdp",
        scatter_dimension=0,
        tiled=True,
    ).astype(jnp.float32)
    query_part, key_part, value_part, out_part, gain_one_part, gain_two_part = (
        lax.psum_scatter(
            contract_rows(normed_one, grad_query_low).astype(jnp.bfloat16),
            "fsdp",
            scatter_dimension=0,
            tiled=True,
        ).astype(jnp.float32),
        lax.psum_scatter(
            contract_rows(normed_one, grad_key_low).astype(jnp.bfloat16),
            "fsdp",
            scatter_dimension=0,
            tiled=True,
        ).astype(jnp.float32),
        lax.psum_scatter(
            contract_rows(normed_one, grad_value_low).astype(jnp.bfloat16),
            "fsdp",
            scatter_dimension=0,
            tiled=True,
        ).astype(jnp.float32),
        lax.psum_scatter(
            contract_rows(mixed_low, grad_attn_low).astype(jnp.bfloat16),
            "fsdp",
            scatter_dimension=0,
            tiled=True,
        ).astype(jnp.float32),
        lax.psum_scatter(
            grad_attn_gain_term.astype(jnp.bfloat16), "fsdp", scatter_dimension=0, tiled=True
        ).astype(jnp.float32),
        lax.psum_scatter(
            grad_ffn_gain_term.astype(jnp.bfloat16), "fsdp", scatter_dimension=0, tiled=True
        ).astype(jnp.float32),
    )
    summed = (
        lax.psum(query_part.astype(jnp.bfloat16), "ctx").astype(jnp.float32),
        lax.psum(key_part.astype(jnp.bfloat16), "ctx").astype(jnp.float32),
        lax.psum(value_part.astype(jnp.bfloat16), "ctx").astype(jnp.float32),
        lax.psum(out_part.astype(jnp.bfloat16), "ctx").astype(jnp.float32),
        lax.psum(gain_one_part.astype(jnp.bfloat16), "ctx").astype(jnp.float32),
        lax.psum(gain_two_part.astype(jnp.bfloat16), "ctx").astype(jnp.float32),
        lax.psum(gate_up_part[:, :ff_cols].astype(jnp.bfloat16), "ctx").astype(jnp.float32),
        lax.psum(gate_up_part[:, ff_cols:].astype(jnp.bfloat16), "ctx").astype(jnp.float32),
        lax.psum(down_part, "ctx").astype(jnp.float32),
    )
    return (
        block_out,
        grad_in,
        summed[4],
        summed[0],
        summed[1],
        summed[2],
        summed[3],
        summed[5],
        summed[6],
        summed[7],
        summed[8],
    )


def solution(mesh):
    placed = (
        P("fsdp", "ctx", None),
        P("fsdp", None),
        P("fsdp"),
        P("fsdp", None),
        P("fsdp", None),
        P("fsdp", None),
        P("fsdp", None),
        P("fsdp"),
        P("fsdp", None),
        P("fsdp", None),
        P("fsdp", None),
        P("fsdp", "ctx", None),
    )
    return jax.shard_map(
        body,
        mesh=mesh,
        in_specs=placed,
        out_specs=(
            P("fsdp", "ctx", None),
            P("fsdp", "ctx", None),
            P("fsdp"),
            P("fsdp", None),
            P("fsdp", None),
            P("fsdp", None),
            P("fsdp", None),
            P("fsdp"),
            P("fsdp", None),
            P("fsdp", None),
            P("fsdp", None),
        ),
        check_vma=False,
    )
```

profile of v0, /device:TPU:1, one launch (start us, length us, event | category | flops | bytes accessed | tf_op | source)
XLA Modules:
  0.0 1085.7 jit_solution(4174884905385580520)
XLA Ops:
  8.0 10.5 all-gather.1
  30.4 16.7 %all-gather = bf16[2,480,320]{1,2,0:T(8,128)(2,1)S(1)} all-gather(bf16[1,480,320]{1,2,0:T(8,128)(2,1)S(1)} %bitcast.459), channel_id=1, replica_groups=mesh['ctx'=16,'fsdp'=2] {'fsdp'}, dimensions={0}, use_global_device_ids=true | all-gather | bytes 921600 | tf_op jit(solution)/shard_map/all_gather | solution.py:209
  57.7 35.7 %all-gather.12.cloned.1.call-done = bf16[2048,320]{1,0:T(8,128)(2,1)} async-done(((bf16[128,320]{1,0:T(8,128)(2,1)}), bf16[2048,320]{1,0:T(8,128)(2,1)}) %all-gather.12.cloned.1.call-update) | async-done | bytes 1310736 | tf_op jit(solution)/shard_map/all_gather | solution.py:245
  95.7 37.1 %all-gather.10.cloned.1.call-done = bf16[2048,320]{0,1:T(8,128)(2,1)} async-done(((bf16[128,320]{0,1:T(8,128)(2,1)}), bf16[2048,320]{0,1:T(8,128)(2,1)}) %all-gather.10.cloned.1.call-update) | async-done | bytes 1310736 | tf_op jit(solution)/shard_map/all_gather | solution.py:246
  142.3 5.9 copy.119
  152.1 5.9 copy.122
  161.9 6.1 while.74
  168.0 4.5 while.72
  173.3 11.1 %while.75 = (s32[]{:T(128)}, f32[64,5,3,64]{0,3,2,1:T(8,128)}, s32[]{:T(128)}, bf16[2048,5,64]{0,2,1:T(8,128)(2,1)S(1)}, s32[64]{0:T(128)S(1)}, /*index=5*/bf16[...) while((s32[]{:T(128)}, f32[64,5,3,64]{0,3,2,1:T(8,128)}, ...), condition=%wide.region_14.16_spmd, body=%wide.region_13.15_spmd.sunk | while | flops 128381448 | bytes 1484215 | solution.py:124
  185.3 8.0 while.73
  198.9 32.1 %all-gather.18.cloned.1.call-done = bf16[960,2560]{1,0:T(8,128)(2,1)} async-done(((bf16[480,2560]{1,0:T(8,128)(2,1)}), bf16[960,2560]{1,0:T(8,128)(2,1)}) %all-gather.18.cloned.1.call-update) | async-done | bytes 4915216 | tf_op jit(solution)/shard_map/all_gather | solution.py:277
  234.3 63.0 %all-gather.20.cloned.1.call-done = bf16[960,2560]{1,0:T(8,128)(2,1)} async-done(((bf16[480,2560]{1,0:T(8,128)(2,1)}), bf16[960,2560]{1,0:T(8,128)(2,1)}) %all-gather.20.cloned.1.call-update) | async-done | bytes 4915216 | tf_op jit(solution)/shard_map/all_gather | solution.py:278
  301.7 62.1 %all-gather.22.cloned.1.call-done = bf16[2560,960]{0,1:T(8,128)(2,1)} async-done(((bf16[1280,960]{0,1:T(8,128)(2,1)}), bf16[2560,960]{0,1:T(8,128)(2,1)}) %all-gather.22.cloned.1.call-update) | async-done | bytes 4915216 | tf_op jit(solution)/shard_map/all_gather | solution.py:287
  363.8 5.0 multiply_convert_fusion
  368.8 4.3 fusion.148
  379.6 16.9 %while.76 = (s32[]{:T(128)}, f32[64,5,3,64]{0,3,2,1:T(8,128)}, f32[2048,5,64]{0,2,1:T(8,128)S(1)}, f32[2048,5,64]{0,2,1:T(8,128)}, s32[]{:T(128)}, /*index=5*/bf...) while((s32[]{:T(128)}, f32[64,5,3,64]{0,3,2,1:T(8,128)}, ...), condition=%wide.region_19.21_spmd, body=%wide.region_18.20_spmd.sunk | while | flops 318927360 | bytes 15605539 | solution.py:180
  396.6 25.2 %while.77 = (s32[]{:T(128)}, f32[64,5,3,64]{0,3,2,1:T(8,128)S(1)}, f32[2048,5,64]{0,2,1:T(8,128)S(1)}, f32[2048,5,64]{0,2,1:T(8,128)}, s32[]{:T(128)}, /*index=5...) while((s32[]{:T(128)}, f32[64,5,3,64]{0,3,2,1:T(8,128)S(1)}, ...), condition=%wide.region_21.23_spmd, body=%wide.region_20.22_spmd.sunk | while | flops 318927360 | bytes 14253831 | solution.py:180
  423.1 4.9 reshape_reshape.14
  428.0 5.4 copy.129
  436.8 5.2 copy.131
  452.8 57.2 %reduce-scatter.25.cloned.1.call-done = bf16[128,320]{1,0:T(8,128)(2,1)} async-done(((bf16[2048,320]{1,0:T(8,128)(2,1)}), bf16[128,320]{1,0:T(8,128)(2,1)}) %reduce-scatter.25.cloned.1.call-update) | async-done | bytes 81936
  512.7 60.4 %reduce-scatter.15.cloned.1.call-done = bf16[128,320]{1,0:T(8,128)(2,1)} async-done(((bf16[2048,320]{1,0:T(8,128)(2,1)}), bf16[128,320]{1,0:T(8,128)(2,1)}) %reduce-scatter.15.cloned.1.call-update) | async-done | bytes 81936 | tf_op jit(solution)/shard_map/reduce_scatter | solution.py:350
  575.8 5.3 convolution_convert_fusion
  595.3 17.9 %reduce-scatter.29.cloned.1.call-done = bf16[480,320]{1,0:T(8,128)(2,1)} async-done(((bf16[960,320]{1,0:T(8,128)(2,1)}), bf16[480,320]{1,0:T(8,128)(2,1)}) %reduce-scatter.29.cloned.1.call-update) | async-done | bytes 307216
  615.1 115.2 %reduce-scatter.21.cloned.1.call-done = bf16[480,5120]{1,0:T(8,128)(2,1)} async-done(((bf16[960,5120]{1,0:T(8,128)(2,1)}), bf16[480,5120]{1,0:T(8,128)(2,1)}) %reduce-scatter.21.cloned.1.call-update) | async-done | bytes 4915216 | tf_op jit(solution)/shard_map/reduce_scatter | solution.py:371
  730.3 5.0 fusion.141
  735.3 28.3 %reduce-scatter.17.cloned.1.call-done = bf16[480,960]{1,0:T(8,128)(2,1)} async-done(((bf16[960,960]{1,0:T(8,128)(2,1)}), bf16[480,960]{1,0:T(8,128)(2,1)}) %reduce-scatter.17.cloned.1.call-update) | async-done | bytes 921616 | tf_op jit(solution)/shard_map/reduce_scatter | solution.py:378
  763.6 33.1 %reduce-scatter.19.cloned.1.call-done = bf16[480,960]{1,0:T(8,128)(2,1)} async-done(((bf16[960,960]{1,0:T(8,128)(2,1)}), bf16[480,960]{1,0:T(8,128)(2,1)}) %reduce-scatter.19.cloned.1.call-update) | async-done | bytes 921616 | tf_op jit(solution)/shard_map/reduce_scatter | solution.py:396
  796.7 65.0 %reduce-scatter.23.cloned.1.call-done = bf16[1280,960]{0,1:T(8,128)(2,1)} async-done(((bf16[2560,960]{0,1:T(8,128)(2,1)}), bf16[1280,960]{0,1:T(8,128)(2,1)}) %reduce-scatter.23.cloned.1.call-update) | async-done | bytes 2457616 | tf_op jit(solution)/shard_map/reduce_scatter | solution.py:368
  862.7 4.6 fusion.100
  873.7 32.3 %all-reduce.4 = (bf16[480]{0:T(512)(128)(2,1)S(1)}, bf16[480]{0:T(512)(128)(2,1)S(1)}) all-reduce(bf16[480]{0:T(512)(128)(2,1)S(1)} %dynamic-slice.3, bf16[480]{0:T(512)(128)(2,1)S(1)} %dynamic-slice.5), channel_id=1, replica_groups=mesh['ctx'=16,'fsdp'=2] {'ctx'}, use_global_device_ids=true, to_apply=%region_27.30 | all-reduce | flops 960 | bytes 3840 | tf_op jit(solution)/shard_map/psum | solution.py:414
  908.1 156.4 %all-reduce.10.cloned.1.call-done = (bf16[480,960]{1,0:T(8,128)(2,1)}, bf16[480,320]{0,1:T(8,128)(2,1)}, bf16[480,320]{0,1:T(8,128)(2,1)}, bf16[480,960]{1,0:T(8...) async-done(((bf16[480,960]{1,0:T(8,128)(2,1)}, bf16[480,320]{0,1:T(8,128)(2,1)}, bf16[480,320]{0,1:T(8,128)(2,1)}, ...) | async-done | bytes 9830416 | tf_op jit(solution)/shard_map/psum | solution.py:410
  (336 shorter events, 180.0 us)
Async XLA Ops:
  7.2 46.3 %all-gather.14.cloned.1.call-start = ((), (), s32[]{:S(2)}) async-start(), calls=%async_computation.10 | async-start | bytes 2949120 | tf_op jit(solution)/shard_map/all_gather | solution.py:207
  7.9 12.0 %copy-start.43 = (u32[32]{0:T(128)S(1)}, u32[32]{0:T(128)}, u32[]{:S(2)}) copy-start(u32[32]{0:T(128)} %constant.165) | copy-start | bytes 388
  7.9 13.4 %copy-start.44 = (bf16[480]{0:T(512)(128)(2,1)S(1)}, bf16[480]{0:T(512)(128)(2,1)}, u32[]{:S(2)}) copy-start(bf16[480]{0:T(512)(128)(2,1)} %param.30) | copy-start | bytes 2884
  7.9 13.6 %copy-start.45 = (bf16[480]{0:T(512)(128)(2,1)S(1)}, bf16[480]{0:T(512)(128)(2,1)}, u32[]{:S(2)}) copy-start(bf16[480]{0:T(512)(128)(2,1)} %param.35) | copy-start | bytes 2884
  7.9 18.1 %copy-start.47 = (s32[1,16]{1,0:T(1,128)S(1)}, s32[1,16]{1,0:T(1,128)}, u32[]{:S(2)}) copy-start(s32[1,16]{1,0:T(1,128)} %param.29) | copy-start | bytes 196
  8.0 20.2 %copy-start.5 = (bf16[1,128,960]{1,2,0:T(8,128)(2,1)S(1)}, bf16[1,128,960]{1,2,0:T(8,128)(2,1)}, u32[]{:S(2)}) copy-start(bf16[1,128,960]{1,2,0:T(8,128)(2,1)} %param.28) | copy-start | bytes 737284
  8.0 85.4 %all-gather.12.cloned.1.call-start = ((), (), s32[]{:S(2)}) async-start(), calls=%async_computation.9 | async-start | bytes 1671168 | tf_op jit(solution)/shard_map/all_gather | solution.py:245
  19.9 27.9 %copy-start.19 = (bf16[960,320]{0,1:T(8,128)(2,1)}, bf16[960,320]{0,1:T(8,128)(2,1)S(1)}, u32[]{:S(2)}) copy-start(bf16[960,320]{0,1:T(8,128)(2,1)S(1)} %reshape.559) | copy-start | bytes 1843204
  30.4 102.5 %all-gather.10.cloned.1.call-start = ((), (), s32[]{:S(2)}) async-start(), calls=%async_computation.8 | async-start | bytes 1392640 | tf_op jit(solution)/shard_map/all_gather | solution.py:246
  49.6 146.5 %all-gather.16.cloned.1.call-start = ((), (), s32[]{:S(2)}) async-start(), calls=%async_computation.11 | async-start | bytes 2949120 | tf_op jit(solution)/shard_map/all_gather | solution.py:210
  50.1 180.9 %all-gather.18.cloned.1.call-start = ((), (), s32[]{:S(2)}) async-start(), calls=%async_computation.12 | async-start | bytes 7372800 | tf_op jit(solution)/shard_map/all_gather | solution.py:277
  50.7 246.6 %all-gather.20.cloned.1.call-start = ((), (), s32[]{:S(2)}) async-start(), calls=%async_computation.13 | async-start | bytes 7372800 | tf_op jit(solution)/shard_map/all_gather | solution.py:278
  51.3 312.5 %all-gather.22.cloned.1.call-start = ((), (), s32[]{:S(2)}) async-start(), calls=%async_computation.14 | async-start | bytes 7372800 | tf_op jit(solution)/shard_map/all_gather | solution.py:287
  52.1 457.9 %reduce-scatter.25.cloned.1.call-start = ((), (), s32[]{:S(2)}) async-start(), calls=%async_computation.20 | async-start | bytes 1671168
  57.4 38.4 %copy-start.11 = (bf16[64,15,64]{0,2,1:T(8,128)(2,1)}, bf16[64,15,64]{0,2,1:T(8,128)(2,1)S(1)}, u32[]{:S(2)}) copy-start(bf16[64,15,64]{0,2,1:T(8,128)(2,1)S(1)} %get-tuple-element.684) | copy-start | bytes 368644
  57.4 38.4 %copy-start.13 = (bf16[64,15,64]{0,2,1:T(8,128)(2,1)}, bf16[64,15,64]{0,2,1:T(8,128)(2,1)S(1)}, u32[]{:S(2)}) copy-start(bf16[64,15,64]{0,2,1:T(8,128)(2,1)S(1)} %get-tuple-element.683) | copy-start | bytes 368644
  198.7 176.1 %copy-start.9 = (f32[128,960]{0,1:T(8,128)}, f32[128,960]{0,1:T(8,128)S(1)}, u32[]{:S(2)}) copy-start(f32[128,960]{0,1:T(8,128)S(1)} %get-tuple-element.710) | copy-start | bytes 1474564
  198.9 98.4 %copy-start.23 = (bf16[128,960]{0,1:T(8,128)(2,1)}, bf16[128,960]{0,1:T(8,128)(2,1)S(1)}, u32[]{:S(2)}) copy-start(bf16[128,960]{0,1:T(8,128)(2,1)S(1)} %multiply_convert_fusion.3) | copy-start | bytes 737284
  234.3 129.5 %copy-start.36 = (bf16[1,128,960]{1,2,0:T(8,128)(2,1)S(1)}, bf16[1,128,960]{1,2,0:T(8,128)(2,1)}, u32[]{:S(2)}) copy-start(bf16[1,128,960]{1,2,0:T(8,128)(2,1)} %param.39) | copy-start | bytes 737284
  452.0 59.1 %copy-start.6 = (bf16[1,128,960]{1,2,0:T(8,128)(2,1)S(1)}, bf16[1,128,960]{1,2,0:T(8,128)(2,1)}, u32[]{:S(2)}) copy-start(bf16[1,128,960]{1,2,0:T(8,128)(2,1)} %param.28) | copy-start | bytes 737284
  452.0 121.2 %reduce-scatter.15.cloned.1.call-start = ((), (), s32[]{:S(2)}) async-start(), calls=%async_computation.15 | async-start | bytes 1671168 | tf_op jit(solution)/shard_map/reduce_scatter | solution.py:350
  452.7 140.7 %reduce-scatter.27.cloned.1.call-start = ((), (), s32[]{:S(2)}) async-start(), calls=%async_computation.21 | async-start | bytes 1105920
  512.7 63.1 %copy-start.24 = (bf16[128,960]{0,1:T(8,128)(2,1)S(1)}, bf16[128,960]{0,1:T(8,128)(2,1)}, u32[]{:S(2)}) copy-start(bf16[128,960]{0,1:T(8,128)(2,1)} %copy-done.23) | copy-start | bytes 737284
  512.7 63.1 %copy-start.27 = (bf16[128,2560]{1,0:T(8,128)(2,1)S(1)}, bf16[128,2560]{1,0:T(8,128)(2,1)}, u32[]{:S(2)}) copy-start(bf16[128,2560]{1,0:T(8,128)(2,1)} %copy-done.26) | copy-start | bytes 1966084
  512.7 63.1 %copy-start.29 = (bf16[128,2560]{1,0:T(8,128)(2,1)S(1)}, bf16[128,2560]{1,0:T(8,128)(2,1)}, u32[]{:S(2)}) copy-start(bf16[128,2560]{1,0:T(8,128)(2,1)} %copy-done.28) | copy-start | bytes 1966084
  512.7 100.6 %reduce-scatter.29.cloned.1.call-start = ((), (), s32[]{:S(2)}) async-start(), calls=%async_computation.22 | async-start | bytes 1105920
  575.7 154.5 %reduce-scatter.21.cloned.1.call-start = ((), (), s32[]{:S(2)}) async-start(), calls=%async_computation.18 | async-start | bytes 14745600 | tf_op jit(solution)/shard_map/reduce_scatter | solution.py:371
  581.2 182.4 %reduce-scatter.17.cloned.1.call-start = ((), (), s32[]{:S(2)}) async-start(), calls=%async_computation.16 | async-start | bytes 2949120 | tf_op jit(solution)/shard_map/reduce_scatter | solution.py:378
  584.5 212.2 %reduce-scatter.19.cloned.1.call-start = ((), (), s32[]{:S(2)}) async-start(), calls=%async_computation.17 | async-start | bytes 2949120 | tf_op jit(solution)/shard_map/reduce_scatter | solution.py:396
  586.6 275.1 %reduce-scatter.23.cloned.1.call-start = ((), (), s32[]{:S(2)}) async-start(), calls=%async_computation.19 | async-start | bytes 7372800 | tf_op jit(solution)/shard_map/reduce_scatter | solution.py:368
  590.5 474.0 %all-reduce.10.cloned.1.call-start = ((), (), s32[]{:S(2)}) async-start(), calls=%async_computation.23 | async-start | bytes 19988480 | tf_op jit(solution)/shard_map/psum | solution.py:410
  868.9 38.2 %copy-start.46 = (f32[128]{0:T(128)S(1)}, f32[128]{0:T(128)}, u32[]{:S(2)}) copy-start(f32[128]{0:T(128)} %get-tuple-element.697) | copy-start | bytes 1540
  (36 other events, 110.1 us)
Sparse Core Ops, SparseCore 0:
  9.6 40.9 all-gather.13
  53.4 39.9 all-gather.11
  96.1 36.6 all-gather.9
  134.2 30.4 all-gather.15
  166.2 64.8 all-gather.17
  232.5 64.8 all-gather.19
  298.9 64.8 all-gather.21
  452.1 57.7 reduce-scatter.24
  514.7 58.4 reduce-scatter.14
  575.9 17.5 reduce-scatter.26
  596.3 16.8 reduce-scatter.28
  615.4 114.7 reduce-scatter.20
  733.2 30.3 reduce-scatter.16
  766.3 30.4 reduce-scatter.18
  799.6 62.0 reduce-scatter.22
  868.2 196.2 all-reduce.9
where the time goes:
time: 1090 us
  waiting for transfers between devices  770 us (71%)
  matrix products  98.3 us (9%)
  local copies, waits for them, and re-layouts  80.7 us (7%)
  blocking collectives  67.6 us (6%)
  other arithmetic  36.9 us (3%)
  between operations  17 us (2%)
  loops' own time  14.1 us (1%)
    psum x1, waiting for transfers between devices, body(): lax.psum(query_part.astype(jnp.bfloat16), 'ctx').astype(jnp.float32)  156 us
    reduce_scatter x1, waiting for transfers between devices, body(): lax.psum_scatter(contract_rows(normed_two, grad_both).astype(jnp.bfloat16...  115 us
    unnamed x19, waiting for transfers between devices  81.8 us
    reduce_scatter x1, waiting for transfers between devices, body(): lax.psum_scatter(contract_rows(hidden, grad_z).astype(jnp.bfloat16), 'fsd...  65 us
    all_gather x1, waiting for transfers between devices, body(): lax.all_gather(w_up, 'fsdp', axis=0, tiled=True)  63 us
    all_gather x1, waiting for transfers between devices, body(): lax.all_gather(w_down, 'fsdp', axis=0, tiled=True)  62.1 us
    reduce_scatter x1, waiting for transfers between devices, body(): lax.psum_scatter(grad_value_dev.astype(jnp.bfloat16), 'ctx', scatter_dime...  60.4 us
    all_gather x1, waiting for transfers between devices, body(): lax.all_gather(value_local, 'ctx', axis=0, tiled=True)  37.1 us
  transfers between devices with their start and end apart: 16, of which 14 were waited for; matrix products, arithmetic and copies ran while one was open for 11% of the time, Pallas kernels for 0%

commit v1 on v0

--- a/solution.py
+++ b/solution.py
@@ -178,6 +178,86 @@
 
     initial = (jnp.zeros(queries.shape, jnp.float32), grad_keys, grad_values)
     return lax.fori_loop(0, tile_count, grad_step, initial)
+
+
+def bit_of(axis_name, bit):
+    return (lax.axis_index(axis_name) >> bit) & 1
+
+
+def swap(array, axis_name, bit):
+    size = lax.axis_size(axis_name)
+    return lax.ppermute(array, axis_name, [(i, i ^ (1 << bit)) for i in range(size)])
+
+
+def bits_of(axis_name):
+    return lax.axis_size(axis_name).bit_length() - 1
+
+
+def half_of(array, index, dim):
+    size = array.shape[dim] // 2
+    return lax.dynamic_slice_in_dim(array, index * size, size, dim)
+
+
+def join(mine, other, bit, dim):
+    first = jnp.where(bit == 0, mine, other)
+    second = jnp.where(bit == 0, other, mine)
+    return jnp.concatenate([first, second], axis=dim)
+
+
+def gather_weight(shard):
+    core = bit_of("ctx", 0)
+    part = half_of(shard, core, 0)[None]
+    size = lax.axis_size("fsdp")
+    pieces = [
+        lax.ppermute(part, "fsdp", [(i, (i + step) % size) for i in range(size)])
+        for step in range(1, size)
+    ]
+    pieces = [join(piece, swap(piece, "ctx", 0), core, 1) for piece in pieces]
+    own = lax.axis_index("fsdp")
+    rows = shard.shape[0]
+    if size == 2:
+        return join(shard, pieces[0][0], own, 0)
+    full = jnp.zeros((size * rows,) + shard.shape[1:], shard.dtype)
+    full = lax.dynamic_update_slice_in_dim(full, shard, own * rows, 0)
+    for step, piece in enumerate(pieces):
+        source = (own - step - 1 + size) % size
+        full = lax.dynamic_update_slice_in_dim(full, piece[0], source * rows, 0)
+    return full
+
+
+def split_dim(shape):
+    rows, columns = shape[1], shape[2]
+    if rows % 16 == 0:
+        return 1
+    if columns % 256 == 0 or rows % 2:
+        return 2
+    return 1 if columns % 2 else 2
+
+
+def reduce_owner(parts, order):
+    trail = []
+    held = parts
+    for axis_name, bit in order:
+        dim = 0 if axis_name == "fsdp" else split_dim(held.shape)
+        own = bit_of(axis_name, bit)
+        other = swap(half_of(held, 1 - own, dim), axis_name, bit)
+        kept = half_of(held, own, dim)
+        held = (kept.astype(jnp.float32) + other.astype(jnp.float32)).astype(jnp.bfloat16)
+        if axis_name == "ctx":
+            trail.append((bit, dim))
+    return held, trail
+
+
+def spread_owner(held, trail):
+    for bit, dim in reversed(trail):
+        held = join(held, swap(held, "ctx", bit), bit_of("ctx", bit), dim)
+    return held
+
+
+def orders():
+    fsdp = [("fsdp", bit) for bit in reversed(range(bits_of("fsdp")))]
+    ctx = [("ctx", bit) for bit in range(1, bits_of("ctx"))]
+    return fsdp, ctx
 
 
 def body(
@@ -203,14 +283,23 @@
     key_span = min(TILE_KEYS, seq_length)
     score_scale = HEAD ** (-0.5)
     group_size = HEADS // KV_HEADS
-    query_full, key_full, value_full, out_full, gain_attn, gain_ffn = (
-        lax.all_gather(w_query, "fsdp", axis=0, tiled=True),
-        lax.all_gather(w_key, "fsdp", axis=0, tiled=True),
-        lax.all_gather(w_value, "fsdp", axis=0, tiled=True),
-        lax.all_gather(w_out, "fsdp", axis=0, tiled=True),
-        lax.all_gather(attn_gain, "fsdp", axis=0, tiled=True),
-        lax.all_gather(ffn_gain, "fsdp", axis=0, tiled=True),
-    )
+    first_bundle = jnp.concatenate(
+        [w_query, w_key, w_value, attn_gain[:, None], ffn_gain[:, None]], axis=1
+    )
+    first_full = gather_weight(first_bundle)
+    kv_size = KV_HEADS * HEAD
+    q_size = HEADS * HEAD
+    qkv_size = q_size + 2 * kv_size
+    qkv_full = first_full[:, :qkv_size]
+    gain_attn = first_full[:, qkv_size]
+    gain_ffn = first_full[:, qkv_size + 1]
+    w_out, w_gate, w_up, w_down, first_full = lax.optimization_barrier(
+        (w_out, w_gate, w_up, w_down, first_full)
+    )
+    out_full = gather_weight(w_out)
+    gate_full = gather_weight(w_gate)
+    up_full = gather_weight(w_up)
+    down_full = gather_weight(w_down)
     gain_attn = gain_attn.astype(jnp.float32)
     gain_ffn = gain_ffn.astype(jnp.float32)
     slot_ids = jnp.arange(pair_total, dtype=jnp.int32)
@@ -222,15 +311,19 @@
     holder = jnp.sum(
         jnp.where(pair_row[None, :] == slot_ids[:, None], slot_ids[None, :], 0), axis=1
     )
-    natural_order = jnp.concatenate([holder * 2, (holder * 2 + 1)[::-1]])
-    device_order = jnp.stack([pair_row, 2 * pair_total - 1 - pair_row], axis=1).reshape(
+    own_slot = lax.axis_index("ctx")
+    relative = holder ^ own_slot
+    natural_order = jnp.concatenate([relative * 2, (relative * 2 + 1)[::-1]])
+    relative_pair = jnp.take(pair_row, slot_ids ^ own_slot)
+    device_order = jnp.stack([relative_pair, 2 * pair_total - 1 - relative_pair], axis=1).reshape(
         2 * pair_total
     )
     inverse_one = inverse_rms(inputs)
     normed_one = (inputs * inverse_one * gain_attn).astype(jnp.bfloat16)
-    query_raw = matmul(normed_one, query_full).reshape(local_rows, HEADS, HEAD)
-    key_raw = matmul(normed_one, key_full).reshape(local_rows, KV_HEADS, HEAD)
-    value_local = matmul(normed_one, value_full).astype(jnp.bfloat16)
+    raw_all = matmul(normed_one, qkv_full)
+    query_raw = raw_all[:, :q_size].reshape(local_rows, HEADS, HEAD)
+    key_raw = raw_all[:, q_size : q_size + kv_size].reshape(local_rows, KV_HEADS, HEAD)
+    value_local = raw_all[:, q_size + kv_size :].astype(jnp.bfloat16)
     queries = (
         rotate(query_raw, cosine_table, sine_table)
         .astype(jnp.bfloat16)
@@ -241,16 +334,17 @@
         .astype(jnp.bfloat16)
         .reshape(local_rows, KV_HEADS * HEAD)
     )
-    key_device, value_device = (
-        lax.all_gather(key_local, "ctx", axis=0, tiled=True),
-        lax.all_gather(value_local, "ctx", axis=0, tiled=True),
-    )
-    keys_natural = reorder_blocks(key_device, natural_order, half_rows).reshape(
-        seq_length, KV_HEADS, HEAD
-    )
-    values_natural = reorder_blocks(value_device, natural_order, half_rows).reshape(
-        seq_length, KV_HEADS, HEAD
-    )
+    ctx_bits = bits_of("ctx")
+    both = jnp.concatenate([key_local, value_local], axis=1)[None]
+    for bit in reversed(range(ctx_bits)):
+        both = jnp.stack([both, swap(both, "ctx", bit)], axis=1).reshape(
+            (2 * both.shape[0],) + both.shape[1:]
+        )
+    both_natural = reorder_blocks(
+        both.reshape(seq_length, 2 * kv_size), natural_order, half_rows
+    )
+    keys_natural = both_natural[:, :kv_size].reshape(seq_length, KV_HEADS, HEAD)
+    values_natural = both_natural[:, kv_size:].reshape(seq_length, KV_HEADS, HEAD)
     tile_counts = (own_blocks * half_rows + half_rows - 1) // key_span + 1
     mixed_parts = []
     stat_parts = []
@@ -273,34 +367,54 @@
     residual = inputs + matmul(mixed_low, out_full)
     inverse_two = inverse_rms(residual)
     normed_two = (residual * inverse_two * gain_ffn).astype(jnp.bfloat16)
-    pieces = (
-        lax.all_gather(w_gate, "fsdp", axis=0, tiled=True),
-        lax.all_gather(w_up, "fsdp", axis=0, tiled=True),
-    )
     columns = normed_two
-    gate_pre = matmul(columns, pieces[0])
-    up_pre = matmul(columns, pieces[1])
+    gate_pre = matmul(columns, gate_full)
+    up_pre = matmul(columns, up_full)
     sigmoid_gate = jax.nn.sigmoid(gate_pre)
     activated = gate_pre * sigmoid_gate
     hidden = (activated * up_pre).astype(jnp.bfloat16)
     columns = hidden
-    down_out = matmul(columns, lax.all_gather(w_down, "fsdp", axis=0, tiled=True))
+    down_out = matmul(columns, down_full)
     block_out = (residual + down_out).astype(jnp.bfloat16)[None]
     grad_z = out_grad[0]
-    grad_hidden = contract_cols(grad_z, lax.all_gather(w_down, "fsdp", axis=0, tiled=True))
+    grad_hidden = contract_cols(grad_z, down_full)
     grad_gate_low = (
         grad_hidden * up_pre * sigmoid_gate * (1.0 + gate_pre * (1.0 - sigmoid_gate))
     ).astype(jnp.bfloat16)
     grad_up_low = (grad_hidden * activated).astype(jnp.bfloat16)
-    pieces = (
-        lax.all_gather(w_gate, "fsdp", axis=0, tiled=True),
-        lax.all_gather(w_up, "fsdp", axis=0, tiled=True),
-    )
-    part = contract_cols(grad_gate_low, pieces[0]) + contract_cols(grad_up_low, pieces[1])
-    grad_both = jnp.concatenate([grad_gate_low, grad_up_low], axis=1)
+    part = contract_cols(grad_gate_low, gate_full) + contract_cols(grad_up_low, up_full)
+    owners = lax.axis_size("fsdp")
+    core = bit_of("ctx", 0)
+    fsdp_order, ctx_order = orders()
+    core_order = [("ctx", 0)]
+
+    def by_owner(left_mat, right_mat):
+        product = contract_rows(left_mat, right_mat).astype(jnp.bfloat16)
+        return product.reshape((owners, product.shape[0] // owners, product.shape[1]))
+
+    down_held, down_trail = reduce_owner(
+        by_owner(hidden, grad_z), core_order + ctx_order + fsdp_order
+    )
+    grad_down = spread_owner(down_held, down_trail)[0].astype(jnp.float32)
+    gate_up_other = swap(
+        by_owner(normed_two, jnp.where(core == 0, grad_up_low, grad_gate_low)), "ctx", 0
+    )
+    gate_up_mine = by_owner(normed_two, jnp.where(core == 0, grad_gate_low, grad_up_low))
+    gate_up = (gate_up_mine.astype(jnp.float32) + gate_up_other.astype(jnp.float32)).astype(
+        jnp.bfloat16
+    )
+    gate_up_held, gate_up_trail = reduce_owner(gate_up, fsdp_order + ctx_order)
+    gate_up_sum = spread_owner(gate_up_held, gate_up_trail)[0]
+    gate_up_peer = swap(gate_up_sum, "ctx", 0)
+    grad_w_gate = jnp.where(core == 0, gate_up_sum, gate_up_peer).astype(jnp.float32)
+    grad_w_up = jnp.where(core == 0, gate_up_peer, gate_up_sum).astype(jnp.float32)
     grad_resid, grad_ffn_gain_term = norm_back(part, residual, inverse_two, gain_ffn)
     grad_resid = grad_resid + grad_z.astype(jnp.float32)
     grad_attn_low = grad_resid.astype(jnp.bfloat16)
+    out_held, out_trail = reduce_owner(
+        by_owner(mixed_low, grad_attn_low), core_order + fsdp_order + ctx_order
+    )
+    grad_w_out = spread_owner(out_held, out_trail)[0].astype(jnp.float32)
     grad_mixed = (
         contract_cols(grad_attn_low, out_full)
         .astype(jnp.bfloat16)
@@ -337,98 +451,58 @@
         .astype(jnp.bfloat16)
         .reshape(local_rows, HEADS * HEAD)
     )
-    grad_key_dev = reorder_blocks(
-        (grad_keys_nat * score_scale).reshape(seq_length, KV_HEADS * HEAD), device_order, half_rows
-    )
-    grad_value_dev = reorder_blocks(
-        grad_values_nat.reshape(seq_length, KV_HEADS * HEAD), device_order, half_rows
-    )
-    key_sum, value_sum = (
-        lax.psum_scatter(
-            grad_key_dev.astype(jnp.bfloat16), "ctx", scatter_dimension=0, tiled=True
-        ).astype(jnp.float32),
-        lax.psum_scatter(
-            grad_value_dev.astype(jnp.bfloat16), "ctx", scatter_dimension=0, tiled=True
-        ).astype(jnp.float32),
-    )
+    grad_both_nat = jnp.concatenate(
+        [
+            (grad_keys_nat * score_scale).reshape(seq_length, kv_size),
+            grad_values_nat.reshape(seq_length, kv_size),
+        ],
+        axis=1,
+    ).astype(jnp.bfloat16)
+    held = reorder_blocks(grad_both_nat, device_order, half_rows).reshape(
+        pair_total, local_rows, 2 * kv_size
+    )
+    for bit in range(ctx_bits):
+        pairs = held.reshape((held.shape[0] // 2, 2) + held.shape[1:])
+        kept = pairs[:, 0].astype(jnp.float32) + swap(pairs[:, 1], "ctx", bit).astype(jnp.float32)
+        held = kept.astype(jnp.bfloat16) if bit < ctx_bits - 1 else kept
+    key_sum = held[0][:, :kv_size]
+    value_sum = held[0][:, kv_size:]
     grad_key_low = (
         unrotate(key_sum.reshape(local_rows, KV_HEADS, HEAD), cosine_table, sine_table)
         .astype(jnp.bfloat16)
         .reshape(local_rows, KV_HEADS * HEAD)
     )
     grad_value_low = value_sum.astype(jnp.bfloat16)
-    grad_normed_one = (
-        contract_cols(grad_query_low, query_full)
-        + contract_cols(grad_key_low, key_full)
-        + contract_cols(grad_value_low, value_full)
-    )
+    grad_qkv_low = jnp.concatenate([grad_query_low, grad_key_low, grad_value_low], axis=1)
+    grad_normed_one = contract_cols(grad_qkv_low, qkv_full)
     grad_inputs, grad_attn_gain_term = norm_back(grad_normed_one, inputs, inverse_one, gain_attn)
     grad_in = (grad_resid + grad_inputs)[None]
-    ff_cols = w_gate.shape[1]
-    down_part = lax.psum_scatter(
-        contract_rows(hidden, grad_z).astype(jnp.bfloat16), "fsdp", scatter_dimension=0, tiled=True
-    )
-    gate_up_part = lax.psum_scatter(
-        contract_rows(normed_two, grad_both).astype(jnp.bfloat16),
-        "fsdp",
-        scatter_dimension=0,
-        tiled=True,
-    ).astype(jnp.float32)
-    query_part, key_part, value_part, out_part, gain_one_part, gain_two_part = (
-        lax.psum_scatter(
-            contract_rows(normed_one, grad_query_low).astype(jnp.bfloat16),
-            "fsdp",
-            scatter_dimension=0,
-            tiled=True,
-        ).astype(jnp.float32),
-        lax.psum_scatter(
-            contract_rows(normed_one, grad_key_low).astype(jnp.bfloat16),
-            "fsdp",
-            scatter_dimension=0,
-            tiled=True,
-        ).astype(jnp.float32),
-        lax.psum_scatter(
-            contract_rows(normed_one, grad_value_low).astype(jnp.bfloat16),
-            "fsdp",
-            scatter_dimension=0,
-            tiled=True,
-        ).astype(jnp.float32),
-        lax.psum_scatter(
-            contract_rows(mixed_low, grad_attn_low).astype(jnp.bfloat16),
-            "fsdp",
-            scatter_dimension=0,
-            tiled=True,
-        ).astype(jnp.float32),
-        lax.psum_scatter(
-            grad_attn_gain_term.astype(jnp.bfloat16), "fsdp", scatter_dimension=0, tiled=True
-        ).astype(jnp.float32),
-        lax.psum_scatter(
-            grad_ffn_gain_term.astype(jnp.bfloat16), "fsdp", scatter_dimension=0, tiled=True
-        ).astype(jnp.float32),
-    )
-    summed = (
-        lax.psum(query_part.astype(jnp.bfloat16), "ctx").astype(jnp.float32),
-        lax.psum(key_part.astype(jnp.bfloat16), "ctx").astype(jnp.float32),
-        lax.psum(value_part.astype(jnp.bfloat16), "ctx").astype(jnp.float32),
-        lax.psum(out_part.astype(jnp.bfloat16), "ctx").astype(jnp.float32),
-        lax.psum(gain_one_part.astype(jnp.bfloat16), "ctx").astype(jnp.float32),
-        lax.psum(gain_two_part.astype(jnp.bfloat16), "ctx").astype(jnp.float32),
-        lax.psum(gate_up_part[:, :ff_cols].astype(jnp.bfloat16), "ctx").astype(jnp.float32),
-        lax.psum(gate_up_part[:, ff_cols:].astype(jnp.bfloat16), "ctx").astype(jnp.float32),
-        lax.psum(down_part, "ctx").astype(jnp.float32),
-    )
+    rows_owned = attn_gain.shape[0]
+    gain_terms = jnp.stack([grad_attn_gain_term, grad_ffn_gain_term], axis=1).astype(jnp.bfloat16)
+    qkv_product = by_owner(normed_one, grad_qkv_low)
+    padding = -(qkv_size + 2) % 256
+    qkv_parts = jnp.concatenate(
+        [
+            qkv_product,
+            gain_terms.reshape(owners, rows_owned, 2),
+            jnp.zeros((owners, rows_owned, padding), jnp.bfloat16),
+        ],
+        axis=2,
+    )
+    qkv_held, qkv_trail = reduce_owner(qkv_parts, core_order + fsdp_order + ctx_order)
+    qkv_sum = spread_owner(qkv_held, qkv_trail)[0].astype(jnp.float32)
     return (
         block_out,
         grad_in,
-        summed[4],
-        summed[0],
-        summed[1],
-        summed[2],
-        summed[3],
-        summed[5],
-        summed[6],
-        summed[7],
-        summed[8],
+        qkv_sum[:, qkv_size],
+        qkv_sum[:, :q_size],
+        qkv_sum[:, q_size : q_size + kv_size],
+        qkv_sum[:, q_size + kv_size : qkv_size],
+        grad_w_out,
+        qkv_sum[:, qkv_size + 1],
+        grad_w_gate,
+        grad_w_up,
+        grad_down,
     )
 
 

time: 1090 us -> 633 us (0.58)
  waiting for transfers between devices: 770 us -> 232 us
  starting transfers between devices: 0.99 us -> 71.3 us
  blocking collectives: 67.6 us -> 0 us
  other arithmetic: 36.9 us -> 88 us
  local copies, waits for them, and re-layouts: 80.7 us -> 126 us
  between operations: 17 us -> 3.1 us
  matrix products: 98.3 us -> 86.7 us
    reduce_scatter x5 -> x0, waiting for transfers between devices: 302 us -> none  [the longest x1 115 us: body(): lax.psum_scatter(contract_rows(normed_two, grad_both).astype(jnp.bfloat16...]
    ppermute x0 -> x54, waiting for transfers between devices: none -> 232 us  [the longest x49 156 us: swap(): lax.ppermute(array, axis_name, [(i, i ^ 1 << bit) for i in range(size)])]
    all_gather x7 -> x0, waiting for transfers between devices: 230 us -> none  [the longest x1 63 us: body(): lax.all_gather(w_up, 'fsdp', axis=0, tiled=True)]
    psum x1 -> x0, waiting for transfers between devices: 156 us -> none  [body(): lax.psum(query_part.astype(jnp.bfloat16), 'ctx').astype(jnp.float32)]
    unnamed x19 -> x0, waiting for transfers between devices: 81.8 us -> none
    ppermute x0 -> x54, starting transfers between devices: none -> 71.3 us  [the longest x49 66.3 us: swap(): lax.ppermute(array, axis_name, [(i, i ^ 1 << bit) for i in range(size)])]
    psum x1 -> x0, blocking collectives: 32.3 us -> none  [body(): lax.psum(gain_one_part.astype(jnp.bfloat16), 'ctx').astype(jnp.float32)]
    concatenate x0 -> x7, local copies, waits for them, and re-layouts: none -> 28.2 us  [the longest x4 18.5 us: body(): jnp.concatenate([(grad_keys_nat * score_scale).reshape(seq_length, kv_siz...]
  transfers between devices with their start and end apart: 16 -> 54, of which waited for: 14 -> 24; matrix products, arithmetic and copies ran while one was open for 11% -> 26% of each run, Pallas kernels for 0% -> 0%
where the time goes in v1:
time: 633 us; the launch traced here: 621 us
  waiting for transfers between devices  232 us (37%)
  local copies, waits for them, and re-layouts  126 us (20%)
  other arithmetic  88 us (14%)
  matrix products  86.7 us (14%)
  starting transfers between devices  71.3 us (11%)
  loops' own time  14.2 us (2%)
    ppermute x49, waiting for transfers between devices, swap(): lax.ppermute(array, axis_name, [(i, i ^ 1 << bit) for i in range(size)])  156 us
    ppermute x5, waiting for transfers between devices, gather_weight(): lax.ppermute(part, 'fsdp', [(i, (i + step) % size) for i in range(size)])  76.1 us
    ppermute x49, starting transfers between devices, swap(): lax.ppermute(array, axis_name, [(i, i ^ 1 << bit) for i in range(size)])  66.3 us
    dynamic_slice x21, local copies, waits for them, and re-layouts, half_of(): return lax.dynamic_slice_in_dim(array, index * size, size, dim)  25.9 us
    select_n x25, other arithmetic, join(): first = jnp.where(bit == 0, mine, other)  25.4 us
    unnamed x159, local copies, waits for them, and re-layouts  18.8 us
    concatenate x4, local copies, waits for them, and re-layouts, body(): jnp.concatenate([(grad_keys_nat * score_scale).reshape(seq_length, kv_siz...  18.5 us
    dot_general x5, matrix products, contract_rows(): lax.dot_general(left_mat, right_mat, (((0,), (0,)), ((), ())), preferred_...  15 us
  transfers between devices with their start and end apart: 54, of which 24 were waited for; matrix products, arithmetic and copies ran while one was open for 26% of the time, Pallas kernels for 0%

profile of v1, /device:TPU:1, one launch (start us, length us, event | category | flops | bytes accessed | tf_op | source)
XLA Modules:
  0.0 620.8 jit_solution(14615290059441579216)
XLA Ops:
  24.6 14.9 %collective-permute-done.6 = bf16[1,240,960]{2,1,0:T(8,128)(2,1)} collective-permute-done((bf16[1,240,960]{2,1,0:T(8,128)(2,1)S(1)}, bf16[1,240,960]{2,1,0:T(8,128)(2,1)}, u32[]{:S(2)}, u32[]{:S(2)}) %collective-permute-start.6) | collective-permute-done | bytes 460832 | tf_op jit(solution)/shard_map/ppermute | solution.py:212
  44.9 47.2 %collective-permute-done.10 = bf16[1,240,2560]{2,1,0:T(8,128)(2,1)} collective-permute-done((bf16[1,240,2560]{2,1,0:T(8,128)(2,1)}, bf16[1,240,2560]{2,1,0:T(8,128)(2,1)}, u32[]{:S(2)}, u32[]{:S(2)}) %collective-permute-start.10) | collective-permute-done | bytes 1228832 | tf_op jit(solution)/shard_map/ppermute | solution.py:212
  104.5 14.0 %collective-permute-done.8 = bf16[1,240,2560]{2,1,0:T(8,128)(2,1)} collective-permute-done((bf16[1,240,2560]{2,1,0:T(8,128)(2,1)}, bf16[1,240,2560]{2,1,0:T(8,128)(2,1)}, u32[]{:S(2)}, u32[]{:S(2)}) %collective-permute-start.8) | collective-permute-done | bytes 1228832 | tf_op jit(solution)/shard_map/ppermute | solution.py:212
  122.0 7.4 %collective-permute-done.3 = bf16[2,128,640]{1,2,0:T(8,128)(2,1)S(1)} collective-permute-done((bf16[2,128,640]{1,2,0:T(8,128)(2,1)S(1)}, bf16[2,128,640]{1,2,0:T(8,128)(2,1)S(1)}, u32[]{:S(2)}, u32[]{:S(2)}) %collective-permute-start.3) | collective-permute-done | bytes 327712 | tf_op jit(solution)/shard_map/ppermute | solution.py:189
  140.4 5.0 collective-permute-done.4
  166.1 6.3 %while.74 = (s32[]{:T(128)}, f32[5,3,64]{2,1,0:T(4,128)S(1)}, f32[5,3,64]{2,1,0:T(4,128)S(1)}, s32[]{:T(128)}, s32[64]{0:T(128)S(1)}, /*index=5*/bf16[2048,5,64]...) while((s32[]{:T(128)}, f32[5,3,64]{2,1,0:T(4,128)S(1)}, ...), condition=%wide.region_12.14_spmd, body=%wide.region_9.13_spmd.sunk | while | flops 66390404 | bytes 4658347 | solution.py:113
  173.3 11.3 %while.75 = (s32[]{:T(128)}, f32[64,5,3,64]{0,3,2,1:T(8,128)}, s32[]{:T(128)}, bf16[2048,5,64]{0,2,1:T(8,128)(2,1)S(1)}, s32[64]{0:T(128)S(1)}, /*index=5*/bf16[...) while((s32[]{:T(128)}, f32[64,5,3,64]{0,3,2,1:T(8,128)}, ...), condition=%wide.region_14.16_spmd, body=%wide.region_13.15_spmd.sunk | while | flops 128381448 | bytes 1484215 | solution.py:124
  184.6 4.5 while.72
  189.9 7.8 %while.73 = (s32[]{:T(128)}, f32[64,5,3,64]{0,3,2,1:T(8,128)}, s32[]{:T(128)}, bf16[2048,5,64]{0,2,1:T(8,128)(2,1)S(1)}, s32[64]{0:T(128)S(1)}, /*index=5*/bf16[...) while((s32[]{:T(128)}, f32[64,5,3,64]{0,3,2,1:T(8,128)}, ...), condition=%wide.region_8.10_spmd, body=%wide.region_7.9_spmd.sunk | while | flops 128381448 | bytes 1484215 | solution.py:124
  217.4 16.9 %while.76 = (s32[]{:T(128)}, f32[64,5,3,64]{0,3,2,1:T(8,128)}, f32[2048,5,64]{0,2,1:T(8,128)S(1)}, f32[2048,5,64]{0,2,1:T(8,128)}, s32[]{:T(128)}, /*index=5*/bf...) while((s32[]{:T(128)}, f32[64,5,3,64]{0,3,2,1:T(8,128)}, ...), condition=%wide.region_19.21_spmd, body=%wide.region_18.20_spmd.sunk | while | flops 318927360 | bytes 15605539 | solution.py:180
  234.4 25.1 %while.77 = (s32[]{:T(128)}, f32[64,5,3,64]{0,3,2,1:T(8,128)S(1)}, f32[2048,5,64]{0,2,1:T(8,128)S(1)}, f32[2048,5,64]{0,2,1:T(8,128)}, s32[]{:T(128)}, /*index=5...) while((s32[]{:T(128)}, f32[64,5,3,64]{0,3,2,1:T(8,128)S(1)}, ...), condition=%wide.region_21.23_spmd, body=%wide.region_20.22_spmd.sunk | while | flops 318927360 | bytes 14253831 | solution.py:180
  262.4 5.1 concatenate.154
  267.5 5.2 copy.254
  277.9 4.4 copy.253
  307.6 11.3 %reshape.570 = bf16[2,1280,960]{1,0,2:T(2,128)(2,1)} reshape(bf16[2560,960]{0,1:T(8,128)(2,1)} %convolution_convert_fusion) | data formatting | bytes 9830400 | tf_op jit(solution)/shard_map/reshape | solution.py:393
  318.9 8.1 %constant_dynamic-slice_fusion.5 = (bf16[2,640,960]{1,0,2:T(2,128)(2,1)}, bf16[2,640,960]{1,0,2:T(2,128)(2,1)}) fusion(bf16[2,1280,960]{1,0,2:T(2,128)(2,1)} %reshape.570, s32[]{:T(128)S(6)} %select_n.537, s32[]{:T(128)S(6)} %select_n.604), kind=kLoop, calls=%fused_computation.352 | loop fusion | bytes 9830408 | tf_op jit(solution)/shard_map/dynamic_slice | solution.py:198
  358.8 5.5 collective-permute-done.15
  377.9 4.0 collective-permute-start.35
  383.0 13.0 %collective-permute-done.46 = bf16[2,320,960]{2,1,0:T(8,128)(2,1)} collective-permute-done((bf16[2,320,960]{2,1,0:T(8,128)(2,1)}, bf16[2,320,960]{2,1,0:T(8,128)(2,1)}, u32[]{:S(2)}, u32[]{:S(2)}) %collective-permute-start.46) | collective-permute-done | bytes 1228832 | tf_op jit(solution)/shard_map/ppermute | solution.py:189
  398.5 5.2 fusion.94
  421.4 5.9 concatenate.158
  438.0 4.8 collective-permute-start.18
  444.8 15.4 %collective-permute-done.48 = bf16[2,80,960]{1,2,0:T(8,128)(2,1)S(1)} collective-permute-done((bf16[2,80,960]{1,2,0:T(8,128)(2,1)S(1)}, bf16[2,80,960]{1,2,0:T(8,128)(2,1)S(1)}, u32[]{:S(2)}, u32[]{:S(2)}) %collective-permute-start.48) | collective-permute-done | bytes 307232 | tf_op jit(solution)/shard_map/ppermute | solution.py:189
  469.5 10.7 %collective-permute-done.50 = bf16[1,80,960]{1,2,0:T(8,128)(2,1)S(1)} collective-permute-done((bf16[1,80,960]{1,2,0:T(8,128)(2,1)S(1)}, bf16[1,80,960]{1,2,0:T(8,128)(2,1)S(1)}, u32[]{:S(2)}, u32[]{:S(2)}) %collective-permute-start.50) | collective-permute-done | bytes 153632 | tf_op jit(solution)/shard_map/ppermute | solution.py:189
  480.5 11.5 %collective-permute-done.38 = bf16[1,240,2560]{2,1,0:T(8,128)(2,1)S(1)} collective-permute-done((bf16[1,240,2560]{2,1,0:T(8,128)(2,1)S(1)}, bf16[1,240,2560]{2,1,0:T(8,128)(2,1)S(1)}, u32[]{:S(2)}, u32[]{:S(2)}) %collective-permute-start.38) | collective-permute-done | bytes 1228832 | tf_op jit(solution)/shard_map/ppermute | solution.py:189
  494.6 11.4 %collective-permute-done.39 = bf16[1,120,2560]{2,1,0:T(8,128)(2,1)S(1)} collective-permute-done((bf16[1,120,2560]{2,1,0:T(8,128)(2,1)S(1)}, bf16[1,120,2560]{2,1,0:T(8,128)(2,1)S(1)}, u32[]{:S(2)}, u32[]{:S(2)}) %collective-permute-start.39) | collective-permute-done | bytes 614432 | tf_op jit(solution)/shard_map/ppermute | solution.py:189
  509.4 14.2 %collective-permute-done.40 = bf16[1,120,1280]{2,1,0:T(8,128)(2,1)S(1)} collective-permute-done((bf16[1,120,1280]{2,1,0:T(8,128)(2,1)}, bf16[1,120,1280]{2,1,0:T(8,128)(2,1)S(1)}, u32[]{:S(2)}, u32[]{:S(2)}) %collective-permute-start.40) | collective-permute-done | bytes 307232 | tf_op jit(solution)/shard_map/ppermute | solution.py:189
  525.1 12.4 %collective-permute-done.41 = bf16[1,120,1280]{2,1,0:T(8,128)(2,1)S(1)} collective-permute-done((bf16[1,120,1280]{2,1,0:T(8,128)(2,1)S(1)}, bf16[1,120,1280]{2,1,0:T(8,128)(2,1)S(1)}, u32[]{:S(2)}, u32[]{:S(2)}) %collective-permute-start.41) | collective-permute-done | bytes 307232 | tf_op jit(solution)/shard_map/ppermute | solution.py:189
  540.9 13.3 %collective-permute-done.22 = bf16[1,120,448]{2,1,0:T(8,128)(2,1)S(1)} collective-permute-done((bf16[1,120,448]{2,1,0:T(8,128)(2,1)S(1)}, bf16[1,120,448]{2,1,0:T(8,128)(2,1)S(1)}, u32[]{:S(2)}, u32[]{:S(2)}) %collective-permute-start.22) | collective-permute-done | bytes 107552 | tf_op jit(solution)/shard_map/ppermute | solution.py:189
  568.3 19.2 %collective-permute-done.43 = bf16[1,240,2560]{2,1,0:T(8,128)(2,1)S(1)} collective-permute-done((bf16[1,240,2560]{2,1,0:T(8,128)(2,1)S(1)}, bf16[1,240,2560]{2,1,0:T(8,128)(2,1)S(1)}, u32[]{:S(2)}, u32[]{:S(2)}) %collective-permute-start.43) | collective-permute-done | bytes 1228832 | tf_op jit(solution)/shard_map/ppermute | solution.py:189
  590.2 4.4 collective-permute-start.44
  613.0 7.6 %select_convert_fusion = (f32[480,2560]{1,0:T(8,128)}, f32[480,2560]{1,0:T(8,128)}) fusion(bf16[480,2560]{1,0:T(8,128)(2,1)} %collective-permute-done.44, pred[]{:T(512)S(6)} %eq.25, bf16[1,240,2560]{2,1,0:T(8,128)(2,1)} %copy-done.11, bf16[1,240,2560]{2,1,0:T(8,128)(2,1)} %copy-done.10), kind=kLoop, calls=%fused_computation.161 | loop fusion | flops 9830400 | bytes 14745601 | tf_op jit(solution)/shard_map/convert_element_type | solution.py:410
  (552 shorter events, 322.4 us)
Async XLA Ops:
  9.0 32.5 %collective-permute-start = (bf16[1,240,1602]{2,1,0:T(8,128)(2,1)}, bf16[1,240,1602]{2,1,0:T(8,128)(2,1)}, u32[]{:S(2)}, u32[]{:S(2)}) collective-permute-start(bf16[1,240,1602]{2,1,0:T(8,128)(2,1)} %dynamic-slice_bitcast_fusion.3), channel_id=1, source_target_pairs={{0,1},{1,0},{2,3},{3,2},{4,5},{5,4},{6,7},{7,6},{8,9},{9,8},{10,11... | collective-permute-start | bytes 2306888 | tf_op jit(solution)/shard_map/ppermute | solution.py:212
  11.1 28.3 %collective-permute-start.6 = (bf16[1,240,960]{2,1,0:T(8,128)(2,1)S(1)}, bf16[1,240,960]{2,1,0:T(8,128)(2,1)}, u32[]{:S(2)}, u32[]{:S(2)}) collective-permute-start(bf16[1,240,960]{2,1,0:T(8,128)(2,1)S(1)} %dynamic-slice_bitcast_fusion.4), channel_id=1, source_target_pairs={{0,1},{1,0},{2,3},{3,2},{4,5},{5,4},{6,7},{7,6},{8,9},{9,8},{10,11... | collective-permute-start | bytes 1382408 | tf_op jit(solution)/shard_map/ppermute | solution.py:212
  13.8 90.4 %collective-permute-start.12 = (bf16[1,640,960]{1,2,0:T(8,128)(2,1)}, bf16[1,640,960]{1,2,0:T(8,128)(2,1)}, u32[]{:S(2)}, u32[]{:S(2)}) collective-permute-start(bf16[1,640,960]{1,2,0:T(8,128)(2,1)} %dynamic-slice_bitcast_fusion), channel_id=1, source_target_pairs={{0,1},{1,0},{2,3},{3,2},{4,5},{5,4},{6,7},{7,6},{8,9},{9,8},{10,11... | collective-permute-start | bytes 3686408 | tf_op jit(solution)/shard_map/ppermute | solution.py:212
  16.3 75.8 %collective-permute-start.10 = (bf16[1,240,2560]{2,1,0:T(8,128)(2,1)}, bf16[1,240,2560]{2,1,0:T(8,128)(2,1)}, u32[]{:S(2)}, u32[]{:S(2)}) collective-permute-start(bf16[1,240,2560]{2,1,0:T(8,128)(2,1)} %dynamic-slice_bitcast_fusion.1), channel_id=1, source_target_pairs={{0,1},{1,0},{2,3},{3,2},{4,5},{5,4},{6,7},{7,6},{8,9},{9,8},{10,11... | collective-permute-start | bytes 3686408 | tf_op jit(solution)/shard_map/ppermute | solution.py:212
  17.5 100.9 %collective-permute-start.8 = (bf16[1,240,2560]{2,1,0:T(8,128)(2,1)}, bf16[1,240,2560]{2,1,0:T(8,128)(2,1)}, u32[]{:S(2)}, u32[]{:S(2)}) collective-permute-start(bf16[1,240,2560]{2,1,0:T(8,128)(2,1)} %dynamic-slice_bitcast_fusion.2), channel_id=1, source_target_pairs={{0,1},{1,0},{2,3},{3,2},{4,5},{5,4},{6,7},{7,6},{8,9},{9,8},{10,11... | collective-permute-start | bytes 3686408 | tf_op jit(solution)/shard_map/ppermute | solution.py:212
  41.5 52.7 %collective-permute-start.1 = (bf16[1,240,1602]{2,1,0:T(8,128)(2,1)}, bf16[1,240,1602]{2,1,0:T(8,128)(2,1)}, u32[]{:S(2)}, u32[]{:S(2)}) collective-permute-start(bf16[1,240,1602]{2,1,0:T(8,128)(2,1)} %collective-permute-done), channel_id=1, source_target_pairs={{0,2},{2,0},{4,6},{6,4},{8,10},{10,8},{12,14},{14,12},{16,18},{18,... | collective-permute-start | bytes 2306888 | tf_op jit(solution)/shard_map/ppermute | solution.py:189
  92.1 39.0 %collective-permute-start.11 = (bf16[1,240,2560]{2,1,0:T(8,128)(2,1)}, bf16[1,240,2560]{2,1,0:T(8,128)(2,1)}, u32[]{:S(2)}, u32[]{:S(2)}) collective-permute-start(bf16[1,240,2560]{2,1,0:T(8,128)(2,1)} %collective-permute-done.10), channel_id=1, source_target_pairs={{0,2},{2,0},{4,6},{6,4},{8,10},{10,8},{12,14},{14,12},{16,18},{18,... | collective-permute-start | bytes 3686408 | tf_op jit(solution)/shard_map/ppermute | solution.py:189
  99.4 20.3 %collective-permute-start.2 = (bf16[1,128,640]{1,2,0:T(8,128)(2,1)S(1)}, bf16[1,128,640]{1,2,0:T(8,128)(2,1)S(1)}, u32[]{:S(2)}, u32[]{:S(2)}) collective-permute-start(bf16[1,128,640]{1,2,0:T(8,128)(2,1)S(1)} %get-tuple-element.881), channel_id=1, source_target_pairs={{0,16},{2,18},{4,20},{6,22},{8,24},{10,26},{12,28},{14,30},{16,0},... | collective-permute-start | bytes 491528 | tf_op jit(solution)/shard_map/ppermute | solution.py:189
  104.2 28.8 %collective-permute-start.13 = (bf16[1,640,960]{1,2,0:T(8,128)(2,1)}, bf16[1,640,960]{1,2,0:T(8,128)(2,1)}, u32[]{:S(2)}, u32[]{:S(2)}) collective-permute-start(bf16[1,640,960]{1,2,0:T(8,128)(2,1)} %collective-permute-done.12), channel_id=1, source_target_pairs={{0,2},{2,0},{4,6},{6,4},{8,10},{10,8},{12,14},{14,12},{16,18},{18,... | collective-permute-start | bytes 3686408 | tf_op jit(solution)/shard_map/ppermute | solution.py:189
  118.5 20.1 %collective-permute-start.9 = (bf16[1,240,2560]{2,1,0:T(8,128)(2,1)}, bf16[1,240,2560]{2,1,0:T(8,128)(2,1)}, u32[]{:S(2)}, u32[]{:S(2)}) collective-permute-start(bf16[1,240,2560]{2,1,0:T(8,128)(2,1)} %collective-permute-done.8), channel_id=1, source_target_pairs={{0,2},{2,0},{4,6},{6,4},{8,10},{10,8},{12,14},{14,12},{16,18},{18,... | collective-permute-start | bytes 3686408 | tf_op jit(solution)/shard_map/ppermute | solution.py:189
  284.5 16.9 %collective-permute-start.27 = (bf16[2,240,960]{2,1,0:T(8,128)(2,1)}, bf16[2,240,960]{2,1,0:T(8,128)(2,1)}, u32[]{:S(2)}, u32[]{:S(2)}) collective-permute-start(bf16[2,240,960]{2,1,0:T(8,128)(2,1)} %constant_dynamic-slice_fusion.14), channel_id=1, source_target_pairs={{0,2},{2,0},{4,6},{6,4},{8,10},{10,8},{12,14},{14,12},{16,18},{18,... | collective-permute-start | bytes 2764808 | tf_op jit(solution)/shard_map/ppermute | solution.py:189
  304.8 22.3 %collective-permute-start.28 = (bf16[1,240,960]{2,1,0:T(8,128)(2,1)}, bf16[1,240,960]{2,1,0:T(8,128)(2,1)}, u32[]{:S(2)}, u32[]{:S(2)}) collective-permute-start(bf16[1,240,960]{2,1,0:T(8,128)(2,1)} %constant_dynamic-slice_fusion.13), channel_id=1, source_target_pairs={{0,1},{1,0},{2,3},{3,2},{4,5},{5,4},{6,7},{7,6},{8,9},{9,8},{10,11... | collective-permute-start | bytes 1382408 | tf_op jit(solution)/shard_map/ppermute | solution.py:189
  307.3 37.2 %collective-permute-start.14 = (bf16[8,128,640]{2,1,0:T(8,128)(2,1)}, bf16[8,128,640]{2,1,0:T(8,128)(2,1)}, u32[]{:S(2)}, u32[]{:S(2)}) collective-permute-start(bf16[8,128,640]{2,1,0:T(8,128)(2,1)} %slice_bitcast_fusion), channel_id=1, source_target_pairs={{0,2},{2,0},{4,6},{6,4},{8,10},{10,8},{12,14},{14,12},{16,18},{18,... | collective-permute-start | bytes 3932168 | tf_op jit(solution)/shard_map/ppermute | solution.py:189
  333.4 65.1 %collective-permute-start.36 = (bf16[2,480,2560]{2,1,0:T(8,128)(2,1)}, bf16[2,480,2560]{2,1,0:T(8,128)(2,1)}, u32[]{:S(2)}, u32[]{:S(2)}) collective-permute-start(bf16[2,480,2560]{2,1,0:T(8,128)(2,1)} %bitcast.121), channel_id=1, source_target_pairs={{0,2},{2,0},{4,6},{6,4},{8,10},{10,8},{12,14},{14,12},{16,18},{18,... | collective-permute-start | bytes 14745608 | tf_op jit(solution)/shard_map/ppermute | solution.py:189
  340.5 24.7 %collective-permute-start.45 = (bf16[2,640,960]{1,2,0:T(8,128)(2,1)S(1)}, bf16[2,640,960]{1,2,0:T(8,128)(2,1)S(1)}, u32[]{:S(2)}, u32[]{:S(2)}) collective-permute-start(bf16[2,640,960]{1,2,0:T(8,128)(2,1)S(1)} %copy.296), channel_id=1, source_target_pairs={{0,2},{2,0},{4,6},{6,4},{8,10},{10,8},{12,14},{14,12},{16,18},{18,... | collective-permute-start | bytes 7372808 | tf_op jit(solution)/shard_map/ppermute | solution.py:189
  357.6 17.7 %collective-permute-start.34 = (bf16[1,120,960]{2,1,0:T(8,128)(2,1)}, bf16[1,120,960]{2,1,0:T(8,128)(2,1)}, u32[]{:S(2)}, u32[]{:S(2)}) collective-permute-start(bf16[1,120,960]{2,1,0:T(8,128)(2,1)} %pad_maximum_fusion.42), channel_id=1, source_target_pairs={{0,4},{2,6},{4,0},{6,2},{8,12},{10,14},{12,8},{14,10},{16,20},{18,... | collective-permute-start | bytes 691208 | tf_op jit(solution)/shard_map/ppermute | solution.py:189
  370.0 25.9 %collective-permute-start.46 = (bf16[2,320,960]{2,1,0:T(8,128)(2,1)}, bf16[2,320,960]{2,1,0:T(8,128)(2,1)}, u32[]{:S(2)}, u32[]{:S(2)}) collective-permute-start(bf16[2,320,960]{2,1,0:T(8,128)(2,1)} %copy.264), channel_id=1, source_target_pairs={{0,4},{2,6},{4,0},{6,2},{8,12},{10,14},{12,8},{14,10},{16,20},{18,... | collective-permute-start | bytes 3686408 | tf_op jit(solution)/shard_map/ppermute | solution.py:189
  377.9 161.8 %collective-permute-start.35 = (bf16[1,240,960]{2,1,0:T(8,128)(2,1)}, bf16[1,240,960]{2,1,0:T(8,128)(2,1)}, u32[]{:S(2)}, u32[]{:S(2)}) collective-permute-start(bf16[1,240,960]{2,1,0:T(8,128)(2,1)} %pad_maximum_fusion.35), channel_id=1, source_target_pairs={{0,2},{2,0},{4,6},{6,4},{8,10},{10,8},{12,14},{14,12},{16,18},{18,... | collective-permute-start | bytes 1382408 | tf_op jit(solution)/shard_map/ppermute | solution.py:189
  406.7 55.1 %collective-permute-start.37 = (bf16[1,480,2560]{2,1,0:T(8,128)(2,1)}, bf16[1,480,2560]{2,1,0:T(8,128)(2,1)}, u32[]{:S(2)}, u32[]{:S(2)}) collective-permute-start(bf16[1,480,2560]{2,1,0:T(8,128)(2,1)} %constant_dynamic-slice_fusion.9), channel_id=1, source_target_pairs={{0,1},{1,0},{2,3},{3,2},{4,5},{5,4},{6,7},{7,6},{8,9},{9,8},{10,11... | collective-permute-start | bytes 7372808 | tf_op jit(solution)/shard_map/ppermute | solution.py:189
  412.5 17.6 %collective-permute-start.47 = (bf16[2,160,960]{2,1,0:T(8,128)(2,1)}, bf16[2,160,960]{2,1,0:T(8,128)(2,1)}, u32[]{:S(2)}, u32[]{:S(2)}) collective-permute-start(bf16[2,160,960]{2,1,0:T(8,128)(2,1)} %copy.266), channel_id=1, source_target_pairs={{0,8},{2,10},{4,12},{6,14},{8,0},{10,2},{12,4},{14,6},{16,24},{18,... | collective-permute-start | bytes 1843208 | tf_op jit(solution)/shard_map/ppermute | solution.py:189
  434.7 25.5 %collective-permute-start.48 = (bf16[2,80,960]{1,2,0:T(8,128)(2,1)S(1)}, bf16[2,80,960]{1,2,0:T(8,128)(2,1)S(1)}, u32[]{:S(2)}, u32[]{:S(2)}) collective-permute-start(bf16[2,80,960]{1,2,0:T(8,128)(2,1)S(1)} %constant_dynamic-slice_fusion.1), channel_id=1, source_target_pairs={{0,16},{2,18},{4,20},{6,22},{8,24},{10,26},{12,28},{14,30},{16,0},... | collective-permute-start | bytes 921608 | tf_op jit(solution)/shard_map/ppermute | solution.py:189
  438.0 27.6 %collective-permute-start.18 = (bf16[2,240,1792]{2,1,0:T(8,128)(2,1)}, bf16[2,240,1792]{2,1,0:T(8,128)(2,1)S(1)}, u32[]{:S(2)}, u32[]{:S(2)}) collective-permute-start(bf16[2,240,1792]{2,1,0:T(8,128)(2,1)} %constant_dynamic-slice_fusion.19), channel_id=1, source_target_pairs={{0,2},{2,0},{4,6},{6,4},{8,10},{10,8},{12,14},{14,12},{16,18},{18,... | collective-permute-start | bytes 5160968 | tf_op jit(solution)/shard_map/ppermute | solution.py:189
  464.4 27.6 %collective-permute-start.38 = (bf16[1,240,2560]{2,1,0:T(8,128)(2,1)S(1)}, bf16[1,240,2560]{2,1,0:T(8,128)(2,1)S(1)}, u32[]{:S(2)}, u32[]{:S(2)}) collective-permute-start(bf16[1,240,2560]{2,1,0:T(8,128)(2,1)S(1)} %constant_dynamic-slice_fusion.8), channel_id=1, source_target_pairs={{0,4},{2,6},{4,0},{6,2},{8,12},{10,14},{12,8},{14,10},{16,20},{18,... | collective-permute-start | bytes 3686408 | tf_op jit(solution)/shard_map/ppermute | solution.py:189
  468.1 24.3 %collective-permute-start.19 = (bf16[1,240,1792]{2,1,0:T(8,128)(2,1)S(1)}, bf16[1,240,1792]{2,1,0:T(8,128)(2,1)S(1)}, u32[]{:S(2)}, u32[]{:S(2)}) collective-permute-start(bf16[1,240,1792]{2,1,0:T(8,128)(2,1)S(1)} %constant_dynamic-slice_fusion.18), channel_id=1, source_target_pairs={{0,1},{1,0},{2,3},{3,2},{4,5},{5,4},{6,7},{7,6},{8,9},{9,8},{10,11... | collective-permute-start | bytes 2580488 | tf_op jit(solution)/shard_map/ppermute | solution.py:189
  480.4 26.4 %collective-permute-start.51 = (bf16[1,160,960]{1,2,0:T(8,128)(2,1)S(1)}, bf16[1,160,960]{1,2,0:T(8,128)(2,1)S(1)}, u32[]{:S(2)}, u32[]{:S(2)}) collective-permute-start(bf16[1,160,960]{1,2,0:T(8,128)(2,1)S(1)} %pad_maximum_fusion.36), channel_id=1, source_target_pairs={{0,8},{2,10},{4,12},{6,14},{8,0},{10,2},{12,4},{14,6},{16,24},{18,... | collective-permute-start | bytes 921608 | tf_op jit(solution)/shard_map/ppermute | solution.py:189
  493.5 30.3 %collective-permute-start.20 = (bf16[1,120,1792]{2,1,0:T(8,128)(2,1)}, bf16[1,120,1792]{2,1,0:T(8,128)(2,1)}, u32[]{:S(2)}, u32[]{:S(2)}) collective-permute-start(bf16[1,120,1792]{2,1,0:T(8,128)(2,1)} %constant_dynamic-slice_fusion.17), channel_id=1, source_target_pairs={{0,4},{2,6},{4,0},{6,2},{8,12},{10,14},{12,8},{14,10},{16,20},{18,... | collective-permute-start | bytes 1290248 | tf_op jit(solution)/shard_map/ppermute | solution.py:189
  508.6 48.9 %collective-permute-start.52 = (bf16[1,320,960]{2,1,0:T(8,128)(2,1)}, bf16[1,320,960]{2,1,0:T(8,128)(2,1)}, u32[]{:S(2)}, u32[]{:S(2)}) collective-permute-start(bf16[1,320,960]{2,1,0:T(8,128)(2,1)} %copy.268), channel_id=1, source_target_pairs={{0,4},{2,6},{4,0},{6,2},{8,12},{10,14},{12,8},{14,10},{16,20},{18,... | collective-permute-start | bytes 1843208 | tf_op jit(solution)/shard_map/ppermute | solution.py:189
  538.4 20.6 %collective-permute-start.42 = (bf16[1,120,2560]{2,1,0:T(8,128)(2,1)}, bf16[1,120,2560]{2,1,0:T(8,128)(2,1)}, u32[]{:S(2)}, u32[]{:S(2)}) collective-permute-start(bf16[1,120,2560]{2,1,0:T(8,128)(2,1)} %pad_maximum_fusion.33), channel_id=1, source_target_pairs={{0,8},{2,10},{4,12},{6,14},{8,0},{10,2},{12,4},{14,6},{16,24},{18,... | collective-permute-start | bytes 1843208 | tf_op jit(solution)/shard_map/ppermute | solution.py:189
  560.4 27.1 %collective-permute-start.43 = (bf16[1,240,2560]{2,1,0:T(8,128)(2,1)S(1)}, bf16[1,240,2560]{2,1,0:T(8,128)(2,1)S(1)}, u32[]{:S(2)}, u32[]{:S(2)}) collective-permute-start(bf16[1,240,2560]{2,1,0:T(8,128)(2,1)S(1)} %pad_maximum_fusion.16), channel_id=1, source_target_pairs={{0,4},{2,6},{4,0},{6,2},{8,12},{10,14},{12,8},{14,10},{16,20},{18,... | collective-permute-start | bytes 3686408 | tf_op jit(solution)/shard_map/ppermute | solution.py:189
  563.2 37.6 %collective-permute-start.53 = (bf16[1,640,960]{1,2,0:T(8,128)(2,1)S(1)}, bf16[1,640,960]{1,2,0:T(8,128)(2,1)S(1)}, u32[]{:S(2)}, u32[]{:S(2)}) collective-permute-start(bf16[1,640,960]{1,2,0:T(8,128)(2,1)S(1)} %pad_maximum_fusion.17), channel_id=1, source_target_pairs={{0,2},{2,0},{4,6},{6,4},{8,10},{10,8},{12,14},{14,12},{16,18},{18,... | collective-permute-start | bytes 3686408 | tf_op jit(solution)/shard_map/ppermute | solution.py:189
  567.6 29.1 %collective-permute-start.25 = (bf16[1,120,1792]{2,1,0:T(8,128)(2,1)S(1)}, bf16[1,120,1792]{2,1,0:T(8,128)(2,1)S(1)}, u32[]{:S(2)}, u32[]{:S(2)}) collective-permute-start(bf16[1,120,1792]{2,1,0:T(8,128)(2,1)S(1)} %pad_maximum_fusion.37), channel_id=1, source_target_pairs={{0,4},{2,6},{4,0},{6,2},{8,12},{10,14},{12,8},{14,10},{16,20},{18,... | collective-permute-start | bytes 1290248 | tf_op jit(solution)/shard_map/ppermute | solution.py:189
  590.2 22.8 %collective-permute-start.44 = (bf16[480,2560]{1,0:T(8,128)(2,1)}, bf16[480,2560]{1,0:T(8,128)(2,1)}, u32[]{:S(2)}, u32[]{:S(2)}) collective-permute-start(bf16[480,2560]{1,0:T(8,128)(2,1)} %maximum_bitcast_fusion.3), channel_id=1, source_target_pairs={{0,2},{2,0},{4,6},{6,4},{8,10},{10,8},{12,14},{14,12},{16,18},{18,... | collective-permute-start | bytes 7372808 | tf_op jit(solution)/shard_map/ppermute | solution.py:189
  (106 other events, 825.1 us)

commit v2 on v1

--- a/solution.py
+++ b/solution.py
@@ -3,6 +3,8 @@
 import jax
 import jax.numpy as jnp
 from jax import lax
+from jax.experimental import pallas as pl
+from jax.experimental.pallas import tpu as pltpu
 from jax.sharding import PartitionSpec as P
 
 HEADS = 15
@@ -13,7 +15,6 @@
 NORM_EPS = 1e-05
 ROPE_BASE = 100000.0
 MASKED = -1e30
-TILE_KEYS = 512
 
 
 def matmul(left_mat, right_mat):
@@ -78,106 +79,137 @@
     return (grad_source, grad_gain)
 
 
-def reorder_blocks(rows_in, block_order, block_rows):
-    blocks = rows_in.reshape((block_order.shape[0], block_rows) + rows_in.shape[1:])
-    return jnp.take(blocks, block_order, axis=0).reshape(rows_in.shape)
-
-
-def tile_scores(queries, key_tile, query_pos, first_key, score_scale):
-    key_span = key_tile.shape[0]
-    scores = (
-        jnp.einsum("qkgd,tkd->kgqt", queries, key_tile, preferred_element_type=jnp.float32)
-        * score_scale
-    )
-    key_pos = first_key + jnp.arange(key_span, dtype=jnp.int32)
-    visible = key_pos[None, None, None, :] <= query_pos[None, None, :, None]
-    return jnp.where(visible, scores, MASKED)
-
-
-def block_forward(
-    queries, query_pos, keys_natural, values_natural, tile_count, key_span, score_scale
+def tie_kernel(value_ref, after_ref, out_ref):
+    del value_ref, after_ref, out_ref
+
+
+def tie(value, after):
+    anywhere = pl.BlockSpec(memory_space=pl.ANY)
+    return pl.pallas_call(
+        tie_kernel,
+        out_shape=jax.ShapeDtypeStruct(value.shape, value.dtype),
+        in_specs=[anywhere, anywhere],
+        out_specs=anywhere,
+        input_output_aliases={0: 0},
+        name="tie",
+    )(value, after)
+
+
+def masked_scores(query_ref, key_ref, query_pos_ref, key_pos_ref):
+    scores = contract_cols(query_ref[0], key_ref[0]) * HEAD ** (-0.5)
+    return jnp.where(key_pos_ref[...] <= query_pos_ref[...], scores, MASKED)
+
+
+def forward_kernel(query_ref, key_ref, value_ref, query_pos_ref, key_pos_ref, mixed_ref, lse_ref):
+    scores = masked_scores(query_ref, key_ref, query_pos_ref, key_pos_ref)
+    row_max = jnp.max(scores, axis=-1, keepdims=True)
+    weights = jnp.exp(scores - row_max)
+    row_sum = jnp.sum(weights, axis=-1, keepdims=True)
+    weights = (weights * (1.0 / row_sum)).astype(jnp.bfloat16)
+    mixed_ref[0] = matmul(weights, value_ref[0])
+    lse_ref[0] = row_max + jnp.log(row_sum)
+
+
+def backward_kernel(
+    query_ref,
+    key_ref,
+    value_ref,
+    query_pos_ref,
+    key_pos_ref,
+    lse_ref,
+    mixed_ref,
+    grad_mixed_ref,
+    after_ref,
+    other_after_ref,
+    grad_query_ref,
+    grad_key_ref,
+    grad_value_ref,
 ):
-    stat_shape = (queries.shape[1], queries.shape[2], queries.shape[0])
-
-    def stats_step(tile_index, running):
-        row_max, row_sum = running
-        key_tile = lax.dynamic_slice_in_dim(keys_natural, tile_index * key_span, key_span, 0)
-        scores = tile_scores(queries, key_tile, query_pos, tile_index * key_span, score_scale)
-        new_max = jnp.maximum(row_max, jnp.max(scores, axis=-1))
-        row_sum = row_sum * jnp.exp(row_max - new_max) + jnp.sum(
-            jnp.exp(scores - new_max[..., None]), axis=-1
-        )
-        return (new_max, row_sum)
-
-    initial = (jnp.full(stat_shape, MASKED, jnp.float32), jnp.zeros(stat_shape, jnp.float32))
-    row_max, row_sum = lax.fori_loop(0, tile_count, stats_step, initial)
-
-    def value_step(tile_index, accumulated):
-        key_tile = lax.dynamic_slice_in_dim(keys_natural, tile_index * key_span, key_span, 0)
-        value_tile = lax.dynamic_slice_in_dim(values_natural, tile_index * key_span, key_span, 0)
-        scores = tile_scores(queries, key_tile, query_pos, tile_index * key_span, score_scale)
-        weights = (jnp.exp(scores - row_max[..., None]) / row_sum[..., None]).astype(jnp.bfloat16)
-        return accumulated + jnp.einsum(
-            "kgqt,tkd->qkgd", weights, value_tile, preferred_element_type=jnp.float32
-        )
-
-    mixed_part = lax.fori_loop(0, tile_count, value_step, jnp.zeros(queries.shape, jnp.float32))
-    return (mixed_part, row_max, row_sum)
-
-
-def block_backward(
-    queries,
-    query_pos,
-    keys_natural,
-    values_natural,
-    tile_count,
-    key_span,
-    score_scale,
-    row_max,
-    row_sum,
-    grad_mixed,
-    row_delta,
-    grad_keys,
-    grad_values,
+    del after_ref, other_after_ref
+    scores = masked_scores(query_ref, key_ref, query_pos_ref, key_pos_ref)
+    probs = jnp.exp(scores - lse_ref[0])
+    grad_mixed = grad_mixed_ref[0]
+    delta = jnp.sum(grad_mixed.astype(jnp.float32) * mixed_ref[0], axis=-1, keepdims=True)
+    grad_value_ref[0] = contract_rows(probs.astype(jnp.bfloat16), grad_mixed).astype(jnp.bfloat16)
+    grad_probs = contract_cols(grad_mixed, value_ref[0])
+    grad_scores = (probs * (grad_probs - delta)).astype(jnp.bfloat16)
+    grad_query_ref[0] = matmul(grad_scores, key_ref[0]) * HEAD ** (-0.5)
+    grad_key_ref[0] = (contract_rows(grad_scores, query_ref[0]) * HEAD ** (-0.5)).astype(
+        jnp.bfloat16
+    )
+
+
+def per_head(rows, columns):
+    return pl.BlockSpec((1, rows, columns), lambda head: (head, 0, 0))
+
+
+def shared(rows, columns):
+    return pl.BlockSpec((rows, columns), lambda head: (0, 0))
+
+
+def attend_forward(queries, keys, values, query_pos, key_pos):
+    heads, rows, _ = queries.shape
+    length = keys.shape[1]
+    return pl.pallas_call(
+        forward_kernel,
+        grid=(heads,),
+        in_specs=[
+            per_head(rows, HEAD),
+            per_head(length, HEAD),
+            per_head(length, HEAD),
+            shared(rows, 1),
+            shared(1, length),
+        ],
+        out_specs=[per_head(rows, HEAD), per_head(rows, 1)],
+        out_shape=[
+            jax.ShapeDtypeStruct((heads, rows, HEAD), jnp.float32),
+            jax.ShapeDtypeStruct((heads, rows, 1), jnp.float32),
+        ],
+        compiler_params=pltpu.CompilerParams(vmem_limit_bytes=50 * 2**20),
+        cost_estimate=pl.CostEstimate(
+            flops=8 * heads * rows * length * HEAD,
+            bytes_accessed=8 * heads * length * HEAD,
+            transcendentals=heads * rows * length,
+        ),
+        name="attend_forward",
+    )(queries, keys, values, query_pos, key_pos)
+
+
+def attend_backward(
+    queries, keys, values, query_pos, key_pos, lse, mixed, grad_mixed, after, other_after
 ):
-
-    def grad_step(tile_index, running):
-        grad_query, key_buffer, value_buffer = running
-        first_key = tile_index * key_span
-        key_tile = lax.dynamic_slice_in_dim(keys_natural, first_key, key_span, 0)
-        value_tile = lax.dynamic_slice_in_dim(values_natural, first_key, key_span, 0)
-        scores = tile_scores(queries, key_tile, query_pos, first_key, score_scale)
-        probs = jnp.exp(scores - row_max[..., None]) / row_sum[..., None]
-        probs_low = probs.astype(jnp.bfloat16)
-        grad_probs = jnp.einsum(
-            "qkgd,tkd->kgqt", grad_mixed, value_tile, preferred_element_type=jnp.float32
-        )
-        grad_scores = (probs * (grad_probs - row_delta[..., None])).astype(jnp.bfloat16)
-        grad_query = grad_query + jnp.einsum(
-            "kgqt,tkd->qkgd", grad_scores, key_tile, preferred_element_type=jnp.float32
-        )
-        key_part = jnp.einsum(
-            "kgqt,qkgd->tkd", grad_scores, queries, preferred_element_type=jnp.float32
-        )
-        value_part = jnp.einsum(
-            "kgqt,qkgd->tkd", probs_low, grad_mixed, preferred_element_type=jnp.float32
-        )
-        key_buffer = lax.dynamic_update_slice_in_dim(
-            key_buffer,
-            lax.dynamic_slice_in_dim(key_buffer, first_key, key_span, 0) + key_part,
-            first_key,
-            0,
-        )
-        value_buffer = lax.dynamic_update_slice_in_dim(
-            value_buffer,
-            lax.dynamic_slice_in_dim(value_buffer, first_key, key_span, 0) + value_part,
-            first_key,
-            0,
-        )
-        return (grad_query, key_buffer, value_buffer)
-
-    initial = (jnp.zeros(queries.shape, jnp.float32), grad_keys, grad_values)
-    return lax.fori_loop(0, tile_count, grad_step, initial)
+    heads, rows, _ = queries.shape
+    length = keys.shape[1]
+    anywhere = pl.BlockSpec(memory_space=pl.ANY)
+    return pl.pallas_call(
+        backward_kernel,
+        grid=(heads,),
+        in_specs=[
+            per_head(rows, HEAD),
+            per_head(length, HEAD),
+            per_head(length, HEAD),
+            shared(rows, 1),
+            shared(1, length),
+            per_head(rows, 1),
+            per_head(rows, HEAD),
+            per_head(rows, HEAD),
+            anywhere,
+            anywhere,
+        ],
+        out_specs=[per_head(rows, HEAD), per_head(length, HEAD), per_head(length, HEAD)],
+        out_shape=[
+            jax.ShapeDtypeStruct((heads, rows, HEAD), jnp.float32),
+            jax.ShapeDtypeStruct((heads, length, HEAD), jnp.bfloat16),
+            jax.ShapeDtypeStruct((heads, length, HEAD), jnp.bfloat16),
+        ],
+        compiler_params=pltpu.CompilerParams(vmem_limit_bytes=50 * 2**20),
+        cost_estimate=pl.CostEstimate(
+            flops=40 * heads * rows * length * HEAD,
+            bytes_accessed=16 * heads * length * HEAD,
+            transcendentals=heads * rows * length,
+        ),
+        name="attend_backward",
+    )(queries, keys, values, query_pos, key_pos, lse, mixed, grad_mixed, after, other_after)
 
 
 def bit_of(axis_name, bit):
@@ -204,9 +236,11 @@
     return jnp.concatenate([first, second], axis=dim)
 
 
-def gather_weight(shard):
+def gather_weight(shard, after=None):
     core = bit_of("ctx", 0)
     part = half_of(shard, core, 0)[None]
+    if after is not None:
+        part = tie(part, after)
     size = lax.axis_size("fsdp")
     pieces = [
         lax.ppermute(part, "fsdp", [(i, (i + step) % size) for i in range(size)])
@@ -280,8 +314,6 @@
     pair_row = pair_of[0]
     pair_total = lax.axis_size("ctx")
     seq_length = pair_total * local_rows
-    key_span = min(TILE_KEYS, seq_length)
-    score_scale = HEAD ** (-0.5)
     group_size = HEADS // KV_HEADS
     first_bundle = jnp.concatenate(
         [w_query, w_key, w_value, attn_gain[:, None], ffn_gain[:, None]], axis=1
@@ -293,13 +325,10 @@
     qkv_full = first_full[:, :qkv_size]
     gain_attn = first_full[:, qkv_size]
     gain_ffn = first_full[:, qkv_size + 1]
-    w_out, w_gate, w_up, w_down, first_full = lax.optimization_barrier(
-        (w_out, w_gate, w_up, w_down, first_full)
-    )
-    out_full = gather_weight(w_out)
-    gate_full = gather_weight(w_gate)
-    up_full = gather_weight(w_up)
-    down_full = gather_weight(w_down)
+    out_full = gather_weight(w_out, first_full)
+    gate_full = gather_weight(w_gate, first_full)
+    up_full = gather_weight(w_up, first_full)
+    down_full = gather_weight(w_down, first_full)
     gain_attn = gain_attn.astype(jnp.float32)
     gain_ffn = gain_ffn.astype(jnp.float32)
     slot_ids = jnp.arange(pair_total, dtype=jnp.int32)
@@ -308,27 +337,30 @@
     offsets = jnp.arange(half_rows, dtype=jnp.int32)
     own_pos = (own_blocks[:, None] * half_rows + offsets[None, :]).reshape(local_rows)
     cosine_table, sine_table = rope_tables(own_pos, HEAD)
-    holder = jnp.sum(
-        jnp.where(pair_row[None, :] == slot_ids[:, None], slot_ids[None, :], 0), axis=1
-    )
-    own_slot = lax.axis_index("ctx")
-    relative = holder ^ own_slot
-    natural_order = jnp.concatenate([relative * 2, (relative * 2 + 1)[::-1]])
-    relative_pair = jnp.take(pair_row, slot_ids ^ own_slot)
-    device_order = jnp.stack([relative_pair, 2 * pair_total - 1 - relative_pair], axis=1).reshape(
-        2 * pair_total
-    )
+    partner = slot_ids ^ lax.axis_index("ctx")
+    relative_pair = jnp.sum(
+        jnp.where(partner[:, None] == slot_ids[None, :], pair_row[None, :], 0), axis=1
+    )
+    relative_blocks = jnp.stack(
+        [relative_pair, 2 * pair_total - 1 - relative_pair], axis=1
+    ).reshape(2 * pair_total)
+    key_pos = (relative_blocks[:, None] * half_rows + offsets[None, :]).reshape(1, seq_length)
+    query_pos = jnp.tile(own_pos, group_size)[:, None]
     inverse_one = inverse_rms(inputs)
     normed_one = (inputs * inverse_one * gain_attn).astype(jnp.bfloat16)
     raw_all = matmul(normed_one, qkv_full)
     query_raw = raw_all[:, :q_size].reshape(local_rows, HEADS, HEAD)
     key_raw = raw_all[:, q_size : q_size + kv_size].reshape(local_rows, KV_HEADS, HEAD)
     value_local = raw_all[:, q_size + kv_size :].astype(jnp.bfloat16)
-    queries = (
-        rotate(query_raw, cosine_table, sine_table)
-        .astype(jnp.bfloat16)
-        .reshape(local_rows, KV_HEADS, group_size, HEAD)
-    )
+    def grouped(rows_in):
+        return jnp.moveaxis(rows_in.reshape(local_rows, HEADS, HEAD), 0, 1).reshape(
+            KV_HEADS, group_size * local_rows, HEAD
+        )
+
+    def ungrouped(heads_in):
+        return jnp.moveaxis(heads_in.reshape(HEADS, local_rows, HEAD), 0, 1)
+
+    queries = grouped(rotate(query_raw, cosine_table, sine_table).astype(jnp.bfloat16))
     key_local = (
         rotate(key_raw, cosine_table, sine_table)
         .astype(jnp.bfloat16)
@@ -340,30 +372,11 @@
         both = jnp.stack([both, swap(both, "ctx", bit)], axis=1).reshape(
             (2 * both.shape[0],) + both.shape[1:]
         )
-    both_natural = reorder_blocks(
-        both.reshape(seq_length, 2 * kv_size), natural_order, half_rows
-    )
-    keys_natural = both_natural[:, :kv_size].reshape(seq_length, KV_HEADS, HEAD)
-    values_natural = both_natural[:, kv_size:].reshape(seq_length, KV_HEADS, HEAD)
-    tile_counts = (own_blocks * half_rows + half_rows - 1) // key_span + 1
-    mixed_parts = []
-    stat_parts = []
-    for half_index in range(2):
-        low_row = half_index * half_rows
-        high_row = low_row + half_rows
-        mixed_part, row_max, row_sum = block_forward(
-            queries[low_row:high_row],
-            own_pos[low_row:high_row],
-            keys_natural,
-            values_natural,
-            tile_counts[half_index],
-            key_span,
-            score_scale,
-        )
-        mixed_parts.append(mixed_part)
-        stat_parts.append((row_max, row_sum))
-    mixed_full = jnp.concatenate(mixed_parts, axis=0)
-    mixed_low = mixed_full.reshape(local_rows, HEADS * HEAD).astype(jnp.bfloat16)
+    both_heads = jnp.moveaxis(both.reshape(seq_length, 2 * KV_HEADS, HEAD), 0, 1)
+    keys = both_heads[:KV_HEADS]
+    values = both_heads[KV_HEADS:]
+    mixed_full, lse = attend_forward(queries, keys, values, query_pos, key_pos)
+    mixed_low = ungrouped(mixed_full).reshape(local_rows, q_size).astype(jnp.bfloat16)
     residual = inputs + matmul(mixed_low, out_full)
     inverse_two = inverse_rms(residual)
     normed_two = (residual * inverse_two * gain_ffn).astype(jnp.bfloat16)
@@ -392,8 +405,9 @@
         product = contract_rows(left_mat, right_mat).astype(jnp.bfloat16)
         return product.reshape((owners, product.shape[0] // owners, product.shape[1]))
 
+    down_product = by_owner(hidden, grad_z)
     down_held, down_trail = reduce_owner(
-        by_owner(hidden, grad_z), core_order + ctx_order + fsdp_order
+        down_product, core_order + fsdp_order + ctx_order
     )
     grad_down = spread_owner(down_held, down_trail)[0].astype(jnp.float32)
     gate_up_other = swap(
@@ -403,8 +417,13 @@
     gate_up = (gate_up_mine.astype(jnp.float32) + gate_up_other.astype(jnp.float32)).astype(
         jnp.bfloat16
     )
-    gate_up_held, gate_up_trail = reduce_owner(gate_up, fsdp_order + ctx_order)
-    gate_up_sum = spread_owner(gate_up_held, gate_up_trail)[0]
+    ff_half = gate_up.shape[2] // 2
+    gate_up_sums = []
+    for part_index, part_order in enumerate((fsdp_order + ctx_order, ctx_order + fsdp_order)):
+        columns = gate_up[:, :, part_index * ff_half : (part_index + 1) * ff_half]
+        gate_up_held, gate_up_trail = reduce_owner(columns, part_order)
+        gate_up_sums.append(spread_owner(gate_up_held, gate_up_trail)[0])
+    gate_up_sum = jnp.concatenate(gate_up_sums, axis=1)
     gate_up_peer = swap(gate_up_sum, "ctx", 0)
     grad_w_gate = jnp.where(core == 0, gate_up_sum, gate_up_peer).astype(jnp.float32)
     grad_w_up = jnp.where(core == 0, gate_up_peer, gate_up_sum).astype(jnp.float32)
@@ -415,50 +434,26 @@
         by_owner(mixed_low, grad_attn_low), core_order + fsdp_order + ctx_order
     )
     grad_w_out = spread_owner(out_held, out_trail)[0].astype(jnp.float32)
-    grad_mixed = (
-        contract_cols(grad_attn_low, out_full)
-        .astype(jnp.bfloat16)
-        .reshape(local_rows, KV_HEADS, group_size, HEAD)
-    )
-    delta_all = jnp.moveaxis(jnp.sum(grad_mixed.astype(jnp.float32) * mixed_full, axis=-1), 0, -1)
-    zero_keys = jnp.zeros((seq_length, KV_HEADS, HEAD), jnp.float32)
-    grad_keys_nat, grad_values_nat = (zero_keys, zero_keys)
-    query_grads = []
-    for half_index in range(2):
-        low_row = half_index * half_rows
-        high_row = low_row + half_rows
-        grad_query_part, grad_keys_nat, grad_values_nat = block_backward(
-            queries[low_row:high_row],
-            own_pos[low_row:high_row],
-            keys_natural,
-            values_natural,
-            tile_counts[half_index],
-            key_span,
-            score_scale,
-            stat_parts[half_index][0],
-            stat_parts[half_index][1],
-            grad_mixed[low_row:high_row],
-            delta_all[..., low_row:high_row],
-            grad_keys_nat,
-            grad_values_nat,
-        )
-        query_grads.append(grad_query_part)
-    grad_query_rot = (jnp.concatenate(query_grads, axis=0) * score_scale).reshape(
-        local_rows, HEADS, HEAD
-    )
+    grad_mixed = grouped(contract_cols(grad_attn_low, out_full).astype(jnp.bfloat16))
+    grad_queries, grad_keys, grad_values = attend_backward(
+        queries,
+        keys,
+        values,
+        query_pos,
+        key_pos,
+        lse,
+        mixed_full,
+        grad_mixed,
+        gate_up,
+        down_product,
+    )
+    grad_query_rot = ungrouped(grad_queries)
     grad_query_low = (
         unrotate(grad_query_rot, cosine_table, sine_table)
         .astype(jnp.bfloat16)
         .reshape(local_rows, HEADS * HEAD)
     )
-    grad_both_nat = jnp.concatenate(
-        [
-            (grad_keys_nat * score_scale).reshape(seq_length, kv_size),
-            grad_values_nat.reshape(seq_length, kv_size),
-        ],
-        axis=1,
-    ).astype(jnp.bfloat16)
-    held = reorder_blocks(grad_both_nat, device_order, half_rows).reshape(
+    held = jnp.moveaxis(jnp.concatenate([grad_keys, grad_values], axis=0), 0, 1).reshape(
         pair_total, local_rows, 2 * kv_size
     )
     for bit in range(ctx_bits):

time: 633 us -> 669 us (1.057)
  matrix products: 86.7 us -> 35.7 us
  Pallas kernels: 0 us -> 28.9 us
  waiting for transfers between devices: 232 us -> 254 us
  local copies, waits for them, and re-layouts: 126 us -> 144 us
  starting transfers between devices: 71.3 us -> 87.4 us
  other arithmetic: 88 us -> 104 us
  loops' own time: 14.2 us -> 0 us
    dot_general x35 -> x0, matrix products: 53.1 us -> none  [the longest x5 14 us: value_step(): jnp.einsum('kgqt,tkd->qkgd', weights, value_tile, preferred_element_type=...]
    ppermute x49 -> x56, waiting for transfers between devices: 156 us -> 186 us  [swap(): lax.ppermute(array, axis_name, [(i, i ^ 1 << bit) for i in range(size)])]
    pallas_call x0 -> x6, Pallas kernels: none -> 28.9 us  [the longest x1 14.9 us: attend_backward(): pl.pallas_call(backward_kernel, grid=(heads,), in_specs=[per_head(rows, H...]
    concatenate x4 -> x0, local copies, waits for them, and re-layouts: 18.5 us -> none  [body(): jnp.concatenate([(grad_keys_nat * score_scale).reshape(seq_length, kv_siz...]
    ppermute x49 -> x56, starting transfers between devices: 66.3 us -> 81.4 us  [swap(): lax.ppermute(array, axis_name, [(i, i ^ 1 << bit) for i in range(size)])]
    another operation x6 -> x0, loops' own time: 14.2 us -> none  [the longest x2 4.83 us: block_backward(): return lax.fori_loop(0, tile_count, grad_step, initial)]
    another operation x10 -> x3, local copies, waits for them, and re-layouts: 2.73 us -> 13.9 us  [the longest x2 8.39 us: body(): both.reshape(seq_length, 2 * KV_HEADS, HEAD)]
    convert_element_type x19 -> x23, other arithmetic: 11.8 us -> 22.3 us  [reduce_owner(): (kept.astype(jnp.float32) + other.astype(jnp.float32)).astype(jnp.bfloat16)]
  transfers between devices with their start and end apart: 54 -> 61, of which waited for: 24 -> 27; matrix products, arithmetic and copies ran while one was open for 26% -> 37% of each run, Pallas kernels for 0% -> 4%
where the time goes in v2:
time: 669 us; the launch traced here: 657 us
  waiting for transfers between devices  254 us (38%)
  local copies, waits for them, and re-layouts  144 us (22%)
  other arithmetic  104 us (16%)
  starting transfers between devices  87.4 us (13%)
  matrix products  35.7 us (5%)
  Pallas kernels  28.9 us (4%)
    ppermute x56, waiting for transfers between devices, swap(): lax.ppermute(array, axis_name, [(i, i ^ 1 << bit) for i in range(size)])  186 us
    ppermute x56, starting transfers between devices, swap(): lax.ppermute(array, axis_name, [(i, i ^ 1 << bit) for i in range(size)])  81.4 us
    ppermute x5, waiting for transfers between devices, gather_weight(): lax.ppermute(part, 'fsdp', [(i, (i + step) % size) for i in range(size)])  68.4 us
    unnamed x143, local copies, waits for them, and re-layouts  27.5 us
    dynamic_slice x27, local copies, waits for them, and re-layouts, half_of(): return lax.dynamic_slice_in_dim(array, index * size, size, dim)  26.7 us
    select_n x27, other arithmetic, join(): first = jnp.where(bit == 0, mine, other)  25.1 us
    convert_element_type x23, other arithmetic, reduce_owner(): (kept.astype(jnp.float32) + other.astype(jnp.float32)).astype(jnp.bfloat16)  22.3 us
    dot_general x5, matrix products, contract_rows(): lax.dot_general(left_mat, right_mat, (((0,), (0,)), ((), ())), preferred_...  14.9 us
  transfers between devices with their start and end apart: 61, of which 27 were waited for; matrix products, arithmetic and copies ran while one was open for 37% of the time, Pallas kernels for 4%

profile of v2, /device:TPU:1, one launch (start us, length us, event | category | flops | bytes accessed | tf_op | source)
XLA Modules:
  0.0 657.1 jit_solution(12501010565409865692)
XLA Ops:
  11.9 15.0 %collective-permute-done = bf16[1,240,1602]{2,1,0:T(8,128)(2,1)S(1)} collective-permute-done((bf16[1,240,1602]{2,1,0:T(8,128)(2,1)S(1)}, bf16[1,240,1602]{2,1,0:T(8,128)(2,1)S(1)}, u32[]{:S(2)}, u32[]{:S(2)}) %collective-permute-start) | collective-permute-done | bytes 768992 | tf_op jit(solution)/shard_map/ppermute | solution.py:246
  38.3 8.0 %collective-permute-done.2 = bf16[1,128,640]{1,2,0:T(8,128)(2,1)S(1)} collective-permute-done((bf16[1,128,640]{1,2,0:T(8,128)(2,1)S(1)}, bf16[1,128,640]{1,2,0:T(8,128)(2,1)S(1)}, u32[]{:S(2)}, u32[]{:S(2)}) %collective-permute-start.2) | collective-permute-done | bytes 163872 | tf_op jit(solution)/shard_map/ppermute | solution.py:221
  48.3 6.7 %collective-permute-done.3 = bf16[2,128,640]{1,2,0:T(8,128)(2,1)S(1)} collective-permute-done((bf16[2,128,640]{1,2,0:T(8,128)(2,1)S(1)}, bf16[2,128,640]{1,2,0:T(8,128)(2,1)S(1)}, u32[]{:S(2)}, u32[]{:S(2)}) %collective-permute-start.3) | collective-permute-done | bytes 327712 | tf_op jit(solution)/shard_map/ppermute | solution.py:221
  86.5 14.0 %collective-permute-done.12 = bf16[1,640,960]{1,2,0:T(8,128)(2,1)} collective-permute-done((bf16[1,640,960]{1,2,0:T(8,128)(2,1)}, bf16[1,640,960]{1,2,0:T(8,128)(2,1)}, u32[]{:S(2)}, u32[]{:S(2)}) %collective-permute-start.12) | collective-permute-done | bytes 1228832 | tf_op jit(solution)/shard_map/ppermute | solution.py:246
  108.4 18.4 %collective-permute-done.10 = bf16[1,240,2560]{2,1,0:T(8,128)(2,1)} collective-permute-done((bf16[1,240,2560]{2,1,0:T(8,128)(2,1)}, bf16[1,240,2560]{2,1,0:T(8,128)(2,1)}, u32[]{:S(2)}, u32[]{:S(2)}) %collective-permute-start.10) | collective-permute-done | bytes 1228832 | tf_op jit(solution)/shard_map/ppermute | solution.py:246
  132.2 21.0 %collective-permute-done.8 = bf16[1,240,2560]{2,1,0:T(8,128)(2,1)} collective-permute-done((bf16[1,240,2560]{2,1,0:T(8,128)(2,1)}, bf16[1,240,2560]{2,1,0:T(8,128)(2,1)}, u32[]{:S(2)}, u32[]{:S(2)}) %collective-permute-start.8) | collective-permute-done | bytes 1228832 | tf_op jit(solution)/shard_map/ppermute | solution.py:246
  176.5 14.1 %attend_forward.1 = (f32[5,384,64]{2,1,0:T(8,128)S(1)}, f32[5,384,1]{2,1,0:T(8,128)S(1)}) custom-call(bf16[5,384,64]{2,1,0:T(8,128)(2,1)S(1)} %bitcast.178, bf16[5,2048,64]{2,1,0:T(8,128)(2,1)} %get-tuple-element.98.key_ref, bf16[5,2048,64]{2,1,0:T(8,128)(2,1)} %get-tuple-element.97.value_ref, s32[384,1]{1,0:T(8,128)S(1)} %bitcast.181, ...), custom_call_target="tpu_custom_call" | custom-call | flops 2013265920 | bytes 5242880 | tf_op jit(solution)/shard_map/attend_forward/pallas_call | solution.py:153
  224.7 7.8 %copy.227 = bf16[2560,960]{1,0:T(8,128)(2,1)} copy(bf16[2560,960]{0,1:T(8,128)(2,1)} %convolution_convert_fusion) | data formatting | bytes 9830400 | tf_op jit(solution)/shard_map/convert_element_type | solution.py:405
  245.2 11.9 %collective-permute-done.29 = bf16[1,240,960]{2,1,0:T(8,128)(2,1)} collective-permute-done((bf16[1,240,960]{2,1,0:T(8,128)(2,1)}, bf16[1,240,960]{2,1,0:T(8,128)(2,1)}, u32[]{:S(2)}, u32[]{:S(2)}) %collective-permute-start.29) | collective-permute-done | bytes 460832 | tf_op jit(solution)/shard_map/ppermute | solution.py:221
  259.7 6.2 collective-permute-done.30
  292.4 5.8 collective-permute-done.33
  304.8 13.9 %collective-permute-done.53 = bf16[1,640,960]{1,2,0:T(8,128)(2,1)} collective-permute-done((bf16[1,640,960]{1,2,0:T(8,128)(2,1)}, bf16[1,640,960]{1,2,0:T(8,128)(2,1)}, u32[]{:S(2)}, u32[]{:S(2)}) %collective-permute-start.53) | collective-permute-done | bytes 1228832 | tf_op jit(solution)/shard_map/ppermute | solution.py:221
  330.1 7.7 %collective-permute-done.54 = bf16[1,320,960]{2,1,0:T(8,128)(2,1)S(1)} collective-permute-done((bf16[1,320,960]{2,1,0:T(8,128)(2,1)S(1)}, bf16[1,320,960]{2,1,0:T(8,128)(2,1)S(1)}, u32[]{:S(2)}, u32[]{:S(2)}) %collective-permute-start.54) | collective-permute-done | bytes 614432 | tf_op jit(solution)/shard_map/ppermute | solution.py:221
  354.8 7.4 %fusion.after_ref = bf16[2,480,2560]{2,1,0:T(8,128)(2,1)} fusion(bf16[2,480,2560]{2,1,0:T(8,128)(2,1)} %bitcast.183, bf16[2,480,2560]{2,1,0:T(8,128)(2,1)} %collective-permute-done.14), kind=kLoop, calls=%fused_computation.1 | loop fusion | flops 9830400 | bytes 14745600 | tf_op jit(solution)/shard_map/convert_element_type | solution.py:417
  362.2 14.9 %attend_backward.1 = (f32[5,384,64]{2,1,0:T(8,128)S(1)}, bf16[5,2048,64]{2,1,0:T(8,128)(2,1)}, bf16[5,2048,64]{2,1,0:T(8,128)(2,1)}) custom-call(bf16[5,384,64]{2,1,0:T(8,128)(2,1)S(1)} %bitcast.179, bf16[5,2048,64]{2,1,0:T(8,128)(2,1)} %get-tuple-element.98.key_ref, bf16[5,2048,64]{2,1,0:T(8,128)(2,1)} %get-tuple-element.97.value_ref, ...), custom_call_target="tpu_custom_call" | custom-call | flops 10066329600 | bytes 10485760 | tf_op jit(solution)/shard_map/attend_backward/pallas_call | solution.py:184
  377.1 5.9 maximum_bitcast_fusion
  382.9 6.1 copy.230
  389.0 5.5 reshape_reshape.7
  394.5 8.0 %fusion.67 = (bf16[8,1,128,640]{2,1,0,3:T(2,128)(2,1)S(1)}, f32[8,1,128,640]{2,1,0,3:T(1,128)}) fusion(bf16[8,2,128,640]{2,1,0,3:T(2,128)(2,1)} %reshape_reshape.7), kind=kLoop, calls=%fused_computation.281 | loop fusion | flops 655360 | bytes 6553600 | tf_op jit(solution)/shard_map/slice | solution.py:461
  423.0 37.0 %collective-permute-done.59 = bf16[1,320,960]{2,1,0:T(8,128)(2,1)S(1)} collective-permute-done((bf16[1,320,960]{2,1,0:T(8,128)(2,1)S(1)}, bf16[1,320,960]{2,1,0:T(8,128)(2,1)S(1)}, u32[]{:S(2)}, u32[]{:S(2)}) %collective-permute-start.59) | collective-permute-done | bytes 614432 | tf_op jit(solution)/shard_map/ppermute | solution.py:221
  493.0 9.2 %collective-permute-done.16 = bf16[4,128,640]{2,1,0:T(8,128)(2,1)} collective-permute-done((bf16[4,128,640]{2,1,0:T(8,128)(2,1)}, bf16[4,128,640]{2,1,0:T(8,128)(2,1)}, u32[]{:S(2)}, u32[]{:S(2)}) %collective-permute-start.16) | collective-permute-done | bytes 655392 | tf_op jit(solution)/shard_map/ppermute | solution.py:221
  519.5 13.5 %collective-permute-done.18 = bf16[1,128,640]{1,2,0:T(8,128)(2,1)S(1)} collective-permute-done((bf16[1,128,640]{1,2,0:T(8,128)(2,1)S(1)}, bf16[1,128,640]{1,2,0:T(8,128)(2,1)S(1)}, u32[]{:S(2)}, u32[]{:S(2)}) %collective-permute-start.18) | collective-permute-done | bytes 163872 | tf_op jit(solution)/shard_map/ppermute | solution.py:221
  538.0 6.1 concatenate.143
  552.6 5.6 collective-permute-done.41
  569.8 7.3 %collective-permute-done.50 = bf16[1,240,1280]{2,1,0:T(8,128)(2,1)S(1)} collective-permute-done((bf16[1,240,1280]{2,1,0:T(8,128)(2,1)S(1)}, bf16[1,240,1280]{2,1,0:T(8,128)(2,1)S(1)}, u32[]{:S(2)}, u32[]{:S(2)}) %collective-permute-start.50) | collective-permute-done | bytes 614432 | tf_op jit(solution)/shard_map/ppermute | solution.py:221
  577.3 5.6 collective-permute-done.20
  584.5 5.8 collective-permute-done.43
  590.5 9.0 %collective-permute-done.21 = bf16[1,120,1792]{2,1,0:T(8,128)(2,1)S(1)} collective-permute-done((bf16[1,120,1792]{2,1,0:T(8,128)(2,1)S(1)}, bf16[1,120,1792]{2,1,0:T(8,128)(2,1)S(1)}, u32[]{:S(2)}, u32[]{:S(2)}) %collective-permute-start.21) | collective-permute-done | bytes 430112 | tf_op jit(solution)/shard_map/ppermute | solution.py:221
  612.2 5.7 collective-permute-start.51
  624.5 5.8 copy.248
  633.9 6.7 %collective-permute-done.26 = bf16[1,120,1792]{2,1,0:T(8,128)(2,1)S(1)} collective-permute-done((bf16[1,120,1792]{2,1,0:T(8,128)(2,1)S(1)}, bf16[1,120,1792]{2,1,0:T(8,128)(2,1)S(1)}, u32[]{:S(2)}, u32[]{:S(2)}) %collective-permute-start.26) | collective-permute-done | bytes 430112 | tf_op jit(solution)/shard_map/ppermute | solution.py:221
  644.2 6.9 %select_convert_fusion = (f32[480,2560]{1,0:T(8,128)}, f32[480,2560]{1,0:T(8,128)}) fusion(bf16[480,2560]{1,0:T(8,128)(2,1)} %collective-permute-done.51, pred[]{:T(512)S(6)} %eq.21, bf16[480,1280]{1,0:T(8,128)(2,1)S(1)} %maximum_bitcast_fusion.8, bf16[480,1280]{1,0:T(8,128)(2,1)S(1)} %maximum_bitcast_fusion.7), kind=kLoop, calls=%fused_computation.38 | loop fusion | flops 9830400 | bytes 14745601 | tf_op jit(solution)/shard_map/convert_element_type | solution.py:429
  (442 shorter events, 331.3 us)
Async XLA Ops:
  7.3 19.6 %collective-permute-start = (bf16[1,240,1602]{2,1,0:T(8,128)(2,1)S(1)}, bf16[1,240,1602]{2,1,0:T(8,128)(2,1)S(1)}, u32[]{:S(2)}, u32[]{:S(2)}) collective-permute-start(bf16[1,240,1602]{2,1,0:T(8,128)(2,1)S(1)} %dynamic-slice_bitcast_fusion.2), channel_id=1, source_target_pairs={{0,1},{1,0},{2,3},{3,2},{4,5},{5,4},{6,7},{7,6},{8,9},{9,8},{10,11... | collective-permute-start | bytes 2306888 | tf_op jit(solution)/shard_map/ppermute | solution.py:246
  70.7 29.8 %collective-permute-start.12 = (bf16[1,640,960]{1,2,0:T(8,128)(2,1)}, bf16[1,640,960]{1,2,0:T(8,128)(2,1)}, u32[]{:S(2)}, u32[]{:S(2)}) collective-permute-start(bf16[1,640,960]{1,2,0:T(8,128)(2,1)} %copy.218), channel_id=1, source_target_pairs={{0,1},{1,0},{2,3},{3,2},{4,5},{5,4},{6,7},{7,6},{8,9},{9,8},{10,11... | collective-permute-start | bytes 3686408 | tf_op jit(solution)/shard_map/ppermute | solution.py:246
  71.9 54.9 %collective-permute-start.10 = (bf16[1,240,2560]{2,1,0:T(8,128)(2,1)}, bf16[1,240,2560]{2,1,0:T(8,128)(2,1)}, u32[]{:S(2)}, u32[]{:S(2)}) collective-permute-start(bf16[1,240,2560]{2,1,0:T(8,128)(2,1)} %tie.6), channel_id=1, source_target_pairs={{0,1},{1,0},{2,3},{3,2},{4,5},{5,4},{6,7},{7,6},{8,9},{9,8},{10,11... | collective-permute-start | bytes 3686408 | tf_op jit(solution)/shard_map/ppermute | solution.py:246
  72.2 81.0 %collective-permute-start.8 = (bf16[1,240,2560]{2,1,0:T(8,128)(2,1)}, bf16[1,240,2560]{2,1,0:T(8,128)(2,1)}, u32[]{:S(2)}, u32[]{:S(2)}) collective-permute-start(bf16[1,240,2560]{2,1,0:T(8,128)(2,1)} %tie.5), channel_id=1, source_target_pairs={{0,1},{1,0},{2,3},{3,2},{4,5},{5,4},{6,7},{7,6},{8,9},{9,8},{10,11... | collective-permute-start | bytes 3686408 | tf_op jit(solution)/shard_map/ppermute | solution.py:246
  75.8 80.2 %collective-permute-start.5 = (bf16[8,128,640]{2,1,0:T(8,128)(2,1)}, bf16[8,128,640]{2,1,0:T(8,128)(2,1)}, u32[]{:S(2)}, u32[]{:S(2)}) collective-permute-start(bf16[8,128,640]{2,1,0:T(8,128)(2,1)} %bitcast.22), channel_id=1, source_target_pairs={{0,2},{2,0},{4,6},{6,4},{8,10},{10,8},{12,14},{14,12},{16,18},{18,... | collective-permute-start | bytes 3932168 | tf_op jit(solution)/shard_map/ppermute | solution.py:221
  103.0 91.2 %collective-permute-start.13 = (bf16[1,640,960]{1,2,0:T(8,128)(2,1)}, bf16[1,640,960]{1,2,0:T(8,128)(2,1)}, u32[]{:S(2)}, u32[]{:S(2)}) collective-permute-start(bf16[1,640,960]{1,2,0:T(8,128)(2,1)} %collective-permute-done.12), channel_id=1, source_target_pairs={{0,2},{2,0},{4,6},{6,4},{8,10},{10,8},{12,14},{14,12},{16,18},{18,... | collective-permute-start | bytes 3686408 | tf_op jit(solution)/shard_map/ppermute | solution.py:221
  126.8 75.3 %collective-permute-start.11 = (bf16[1,240,2560]{2,1,0:T(8,128)(2,1)}, bf16[1,240,2560]{2,1,0:T(8,128)(2,1)}, u32[]{:S(2)}, u32[]{:S(2)}) collective-permute-start(bf16[1,240,2560]{2,1,0:T(8,128)(2,1)} %collective-permute-done.10), channel_id=1, source_target_pairs={{0,2},{2,0},{4,6},{6,4},{8,10},{10,8},{12,14},{14,12},{16,18},{18,... | collective-permute-start | bytes 3686408 | tf_op jit(solution)/shard_map/ppermute | solution.py:221
  153.1 50.9 %collective-permute-start.9 = (bf16[1,240,2560]{2,1,0:T(8,128)(2,1)}, bf16[1,240,2560]{2,1,0:T(8,128)(2,1)}, u32[]{:S(2)}, u32[]{:S(2)}) collective-permute-start(bf16[1,240,2560]{2,1,0:T(8,128)(2,1)} %collective-permute-done.8), channel_id=1, source_target_pairs={{0,2},{2,0},{4,6},{6,4},{8,10},{10,8},{12,14},{14,12},{16,18},{18,... | collective-permute-start | bytes 3686408 | tf_op jit(solution)/shard_map/ppermute | solution.py:221
  219.9 21.5 %collective-permute-start.28 = (bf16[2,240,960]{2,1,0:T(8,128)(2,1)}, bf16[2,240,960]{2,1,0:T(8,128)(2,1)}, u32[]{:S(2)}, u32[]{:S(2)}) collective-permute-start(bf16[2,240,960]{2,1,0:T(8,128)(2,1)} %constant_dynamic-slice_fusion.17), channel_id=1, source_target_pairs={{0,2},{2,0},{4,6},{6,4},{8,10},{10,8},{12,14},{14,12},{16,18},{18,... | collective-permute-start | bytes 2764808 | tf_op jit(solution)/shard_map/ppermute | solution.py:221
  240.8 38.2 %collective-permute-start.52 = (bf16[2,640,960]{1,2,0:T(8,128)(2,1)}, bf16[2,640,960]{1,2,0:T(8,128)(2,1)}, u32[]{:S(2)}, u32[]{:S(2)}) collective-permute-start(bf16[2,640,960]{1,2,0:T(8,128)(2,1)} %copy.239), channel_id=1, source_target_pairs={{0,2},{2,0},{4,6},{6,4},{8,10},{10,8},{12,14},{14,12},{16,18},{18,... | collective-permute-start | bytes 7372808 | tf_op jit(solution)/shard_map/ppermute | solution.py:221
  273.0 81.8 %collective-permute-start.14 = (bf16[2,480,2560]{2,1,0:T(8,128)(2,1)}, bf16[2,480,2560]{2,1,0:T(8,128)(2,1)}, u32[]{:S(2)}, u32[]{:S(2)}) collective-permute-start(bf16[2,480,2560]{2,1,0:T(8,128)(2,1)} %bitcast.44), channel_id=1, source_target_pairs={{0,2},{2,0},{4,6},{6,4},{8,10},{10,8},{12,14},{14,12},{16,18},{18,... | collective-permute-start | bytes 14745608 | tf_op jit(solution)/shard_map/ppermute | solution.py:221
  290.1 28.6 %collective-permute-start.53 = (bf16[1,640,960]{1,2,0:T(8,128)(2,1)}, bf16[1,640,960]{1,2,0:T(8,128)(2,1)}, u32[]{:S(2)}, u32[]{:S(2)}) collective-permute-start(bf16[1,640,960]{1,2,0:T(8,128)(2,1)} %copy.241), channel_id=1, source_target_pairs={{0,1},{1,0},{2,3},{3,2},{4,5},{5,4},{6,7},{7,6},{8,9},{9,8},{10,11... | collective-permute-start | bytes 3686408 | tf_op jit(solution)/shard_map/ppermute | solution.py:221
  304.6 22.0 %collective-permute-start.35 = (bf16[1,120,960]{2,1,0:T(8,128)(2,1)}, bf16[1,120,960]{2,1,0:T(8,128)(2,1)}, u32[]{:S(2)}, u32[]{:S(2)}) collective-permute-start(bf16[1,120,960]{2,1,0:T(8,128)(2,1)} %pad_maximum_fusion.42), channel_id=1, source_target_pairs={{0,4},{2,6},{4,0},{6,2},{8,12},{10,14},{12,8},{14,10},{16,20},{18,... | collective-permute-start | bytes 691208 | tf_op jit(solution)/shard_map/ppermute | solution.py:221
  354.7 47.8 %collective-permute-start.57 = (bf16[1,80,960]{2,1,0:T(8,128)(2,1)S(1)}, bf16[1,80,960]{2,1,0:T(8,128)(2,1)}, u32[]{:S(2)}, u32[]{:S(2)}) collective-permute-start(bf16[1,80,960]{2,1,0:T(8,128)(2,1)S(1)} %add_convert_fusion.18), channel_id=1, source_target_pairs={{0,16},{2,18},{4,20},{6,22},{8,24},{10,26},{12,28},{14,30},{16,0},... | collective-permute-start | bytes 460808 | tf_op jit(solution)/shard_map/ppermute | solution.py:221
  409.7 63.2 %collective-permute-start.15 = (bf16[8,128,640]{1,0,2:T(8,128)(2,1)}, bf16[8,128,640]{1,0,2:T(8,128)(2,1)}, u32[]{:S(2)}, u32[]{:S(2)}) collective-permute-start(bf16[8,128,640]{1,0,2:T(8,128)(2,1)} %bitcast.175), channel_id=1, source_target_pairs={{0,2},{2,0},{4,6},{6,4},{8,10},{10,8},{12,14},{14,12},{16,18},{18,... | collective-permute-start | bytes 3932168 | tf_op jit(solution)/shard_map/ppermute | solution.py:221
  417.1 48.4 %collective-permute-start.44 = (bf16[2,240,1280]{2,1,0:T(8,128)(2,1)}, bf16[2,240,1280]{2,1,0:T(8,128)(2,1)}, u32[]{:S(2)}, u32[]{:S(2)}) collective-permute-start(bf16[2,240,1280]{2,1,0:T(8,128)(2,1)} %constant_dynamic-slice_fusion.8), channel_id=1, source_target_pairs={{0,4},{2,6},{4,0},{6,2},{8,12},{10,14},{12,8},{14,10},{16,20},{18,... | collective-permute-start | bytes 3686408 | tf_op jit(solution)/shard_map/ppermute | solution.py:221
  418.5 41.5 %collective-permute-start.59 = (bf16[1,320,960]{2,1,0:T(8,128)(2,1)S(1)}, bf16[1,320,960]{2,1,0:T(8,128)(2,1)S(1)}, u32[]{:S(2)}, u32[]{:S(2)}) collective-permute-start(bf16[1,320,960]{2,1,0:T(8,128)(2,1)S(1)} %pad_maximum_fusion.31), channel_id=1, source_target_pairs={{0,4},{2,6},{4,0},{6,2},{8,12},{10,14},{12,8},{14,10},{16,20},{18,... | collective-permute-start | bytes 1843208 | tf_op jit(solution)/shard_map/ppermute | solution.py:221
  421.0 49.1 %collective-permute-start.37 = (bf16[1,480,1280]{2,1,0:T(8,128)(2,1)}, bf16[1,480,1280]{2,1,0:T(8,128)(2,1)}, u32[]{:S(2)}, u32[]{:S(2)}) collective-permute-start(bf16[1,480,1280]{2,1,0:T(8,128)(2,1)} %constant_dynamic-slice_fusion.12), channel_id=1, source_target_pairs={{0,1},{1,0},{2,3},{3,2},{4,5},{5,4},{6,7},{7,6},{8,9},{9,8},{10,11... | collective-permute-start | bytes 3686408 | tf_op jit(solution)/shard_map/ppermute | solution.py:221
  464.7 40.7 %collective-permute-start.60 = (bf16[1,640,960]{1,2,0:T(8,128)(2,1)}, bf16[1,640,960]{1,2,0:T(8,128)(2,1)}, u32[]{:S(2)}, u32[]{:S(2)}) collective-permute-start(bf16[1,640,960]{1,2,0:T(8,128)(2,1)} %copy.243), channel_id=1, source_target_pairs={{0,2},{2,0},{4,6},{6,4},{8,10},{10,8},{12,14},{14,12},{16,18},{18,... | collective-permute-start | bytes 3686408 | tf_op jit(solution)/shard_map/ppermute | solution.py:221
  468.4 16.3 %collective-permute-start.45 = (bf16[2,120,1280]{2,1,0:T(8,128)(2,1)}, bf16[2,120,1280]{2,1,0:T(8,128)(2,1)}, u32[]{:S(2)}, u32[]{:S(2)}) collective-permute-start(bf16[2,120,1280]{2,1,0:T(8,128)(2,1)} %constant_dynamic-slice_fusion.7), channel_id=1, source_target_pairs={{0,8},{2,10},{4,12},{6,14},{8,0},{10,2},{12,4},{14,6},{16,24},{18,... | collective-permute-start | bytes 1843208 | tf_op jit(solution)/shard_map/ppermute | solution.py:221
  472.7 16.8 %collective-permute-start.38 = (bf16[1,240,1280]{2,1,0:T(8,128)(2,1)}, bf16[1,240,1280]{2,1,0:T(8,128)(2,1)}, u32[]{:S(2)}, u32[]{:S(2)}) collective-permute-start(bf16[1,240,1280]{2,1,0:T(8,128)(2,1)} %constant_dynamic-slice_fusion.11), channel_id=1, source_target_pairs={{0,4},{2,6},{4,0},{6,2},{8,12},{10,14},{12,8},{14,10},{16,20},{18,... | collective-permute-start | bytes 1843208 | tf_op jit(solution)/shard_map/ppermute | solution.py:221
  481.2 21.1 %collective-permute-start.16 = (bf16[4,128,640]{2,1,0:T(8,128)(2,1)}, bf16[4,128,640]{2,1,0:T(8,128)(2,1)}, u32[]{:S(2)}, u32[]{:S(2)}) collective-permute-start(bf16[4,128,640]{2,1,0:T(8,128)(2,1)} %bitcast.55), channel_id=1, source_target_pairs={{0,4},{2,6},{4,0},{6,2},{8,12},{10,14},{12,8},{14,10},{16,20},{18,... | collective-permute-start | bytes 1966088 | tf_op jit(solution)/shard_map/ppermute | solution.py:221
  486.9 22.5 %collective-permute-start.46 = (bf16[2,120,640]{2,1,0:T(8,128)(2,1)}, bf16[2,120,640]{2,1,0:T(8,128)(2,1)S(1)}, u32[]{:S(2)}, u32[]{:S(2)}) collective-permute-start(bf16[2,120,640]{2,1,0:T(8,128)(2,1)} %constant_dynamic-slice_fusion.6), channel_id=1, source_target_pairs={{0,16},{2,18},{4,20},{6,22},{8,24},{10,26},{12,28},{14,30},{16,0},... | collective-permute-start | bytes 921608 | tf_op jit(solution)/shard_map/ppermute | solution.py:221
  491.7 19.1 %collective-permute-start.39 = (bf16[1,120,1280]{2,1,0:T(8,128)(2,1)}, bf16[1,120,1280]{2,1,0:T(8,128)(2,1)}, u32[]{:S(2)}, u32[]{:S(2)}) collective-permute-start(bf16[1,120,1280]{2,1,0:T(8,128)(2,1)} %constant_dynamic-slice_fusion.10), channel_id=1, source_target_pairs={{0,8},{2,10},{4,12},{6,14},{8,0},{10,2},{12,4},{14,6},{16,24},{18,... | collective-permute-start | bytes 921608 | tf_op jit(solution)/shard_map/ppermute | solution.py:221
  512.7 34.7 %collective-permute-start.40 = (bf16[1,120,640]{2,1,0:T(8,128)(2,1)}, bf16[1,120,640]{2,1,0:T(8,128)(2,1)}, u32[]{:S(2)}, u32[]{:S(2)}) collective-permute-start(bf16[1,120,640]{2,1,0:T(8,128)(2,1)} %constant_dynamic-slice_fusion.9), channel_id=1, source_target_pairs={{0,16},{2,18},{4,20},{6,22},{8,24},{10,26},{12,28},{14,30},{16,0},... | collective-permute-start | bytes 460808 | tf_op jit(solution)/shard_map/ppermute | solution.py:221
  516.4 16.7 %collective-permute-start.18 = (bf16[1,128,640]{1,2,0:T(8,128)(2,1)S(1)}, bf16[1,128,640]{1,2,0:T(8,128)(2,1)S(1)}, u32[]{:S(2)}, u32[]{:S(2)}) collective-permute-start(bf16[1,128,640]{1,2,0:T(8,128)(2,1)S(1)} %slice_bitcast_fusion), channel_id=1, source_target_pairs={{0,16},{2,18},{4,20},{6,22},{8,24},{10,26},{12,28},{14,30},{16,0},... | collective-permute-start | bytes 491528 | tf_op jit(solution)/shard_map/ppermute | solution.py:221
  517.4 31.1 %collective-permute-start.48 = (bf16[1,120,640]{2,1,0:T(8,128)(2,1)}, bf16[1,120,640]{2,1,0:T(8,128)(2,1)}, u32[]{:S(2)}, u32[]{:S(2)}) collective-permute-start(bf16[1,120,640]{2,1,0:T(8,128)(2,1)} %add_convert_fusion.19), channel_id=1, source_target_pairs={{0,16},{2,18},{4,20},{6,22},{8,24},{10,26},{12,28},{14,30},{16,0},... | collective-permute-start | bytes 460808 | tf_op jit(solution)/shard_map/ppermute | solution.py:221
  545.7 17.5 %collective-permute-start.19 = (bf16[2,240,1792]{2,1,0:T(8,128)(2,1)S(1)}, bf16[2,240,1792]{2,1,0:T(8,128)(2,1)S(1)}, u32[]{:S(2)}, u32[]{:S(2)}) collective-permute-start(bf16[2,240,1792]{2,1,0:T(8,128)(2,1)S(1)} %constant_dynamic-slice_fusion.22), channel_id=1, source_target_pairs={{0,2},{2,0},{4,6},{6,4},{8,10},{10,8},{12,14},{14,12},{16,18},{18,... | collective-permute-start | bytes 5160968 | tf_op jit(solution)/shard_map/ppermute | solution.py:221
  563.7 19.2 %collective-permute-start.20 = (bf16[1,240,1792]{2,1,0:T(8,128)(2,1)S(1)}, bf16[1,240,1792]{2,1,0:T(8,128)(2,1)S(1)}, u32[]{:S(2)}, u32[]{:S(2)}) collective-permute-start(bf16[1,240,1792]{2,1,0:T(8,128)(2,1)S(1)} %constant_dynamic-slice_fusion.21), channel_id=1, source_target_pairs={{0,1},{1,0},{2,3},{3,2},{4,5},{5,4},{6,7},{7,6},{8,9},{9,8},{10,11... | collective-permute-start | bytes 2580488 | tf_op jit(solution)/shard_map/ppermute | solution.py:221
  569.5 20.8 %collective-permute-start.43 = (bf16[1,240,1280]{2,1,0:T(8,128)(2,1)S(1)}, bf16[1,240,1280]{2,1,0:T(8,128)(2,1)S(1)}, u32[]{:S(2)}, u32[]{:S(2)}) collective-permute-start(bf16[1,240,1280]{2,1,0:T(8,128)(2,1)S(1)} %pad_maximum_fusion.32), channel_id=1, source_target_pairs={{0,4},{2,6},{4,0},{6,2},{8,12},{10,14},{12,8},{14,10},{16,20},{18,... | collective-permute-start | bytes 1843208 | tf_op jit(solution)/shard_map/ppermute | solution.py:221
  583.2 16.3 %collective-permute-start.21 = (bf16[1,120,1792]{2,1,0:T(8,128)(2,1)S(1)}, bf16[1,120,1792]{2,1,0:T(8,128)(2,1)S(1)}, u32[]{:S(2)}, u32[]{:S(2)}) collective-permute-start(bf16[1,120,1792]{2,1,0:T(8,128)(2,1)S(1)} %constant_dynamic-slice_fusion.20), channel_id=1, source_target_pairs={{0,4},{2,6},{4,0},{6,2},{8,12},{10,14},{12,8},{14,10},{16,20},{18,... | collective-permute-start | bytes 1290248 | tf_op jit(solution)/shard_map/ppermute | solution.py:221
  612.2 32.1 %collective-permute-start.51 = (bf16[480,2560]{1,0:T(8,128)(2,1)}, bf16[480,2560]{1,0:T(8,128)(2,1)}, u32[]{:S(2)}, u32[]{:S(2)}) collective-permute-start(bf16[480,2560]{1,0:T(8,128)(2,1)} %pad_maximum_fusion.11), channel_id=1, source_target_pairs={{0,2},{2,0},{4,6},{6,4},{8,10},{10,8},{12,14},{14,12},{16,18},{18,... | collective-permute-start | bytes 7372808 | tf_op jit(solution)/shard_map/ppermute | solution.py:221
  (95 other events, 990.5 us)

commit v3 on v2

--- a/solution.py
+++ b/solution.py
@@ -236,16 +236,22 @@
     return jnp.concatenate([first, second], axis=dim)
 
 
-def gather_weight(shard, after=None):
+def gather_weight(shard):
     core = bit_of("ctx", 0)
     part = half_of(shard, core, 0)[None]
-    if after is not None:
-        part = tie(part, after)
     size = lax.axis_size("fsdp")
     pieces = [
         lax.ppermute(part, "fsdp", [(i, (i + step) % size) for i in range(size)])
         for step in range(1, size)
     ]
+    return pieces
+
+
+def finish_weight(shard, pieces, after=None):
+    core = bit_of("ctx", 0)
+    size = lax.axis_size("fsdp")
+    if after is not None:
+        pieces = [tie(piece, after) for piece in pieces]
     pieces = [join(piece, swap(piece, "ctx", 0), core, 1) for piece in pieces]
     own = lax.axis_index("fsdp")
     rows = shard.shape[0]
@@ -268,15 +274,27 @@
     return 1 if columns % 2 else 2
 
 
-def reduce_owner(parts, order):
+def reduce_open(held, order):
+    axis_name, bit = order[0]
+    dim = 0 if axis_name == "fsdp" else split_dim(held.shape)
+    own = bit_of(axis_name, bit)
+    sent = half_of(held, 1 - own, dim)
+    return half_of(held, own, dim), sent, swap(sent, axis_name, bit), dim
+
+
+def add_low(kept, other):
+    return (kept.astype(jnp.float32) + other.astype(jnp.float32)).astype(jnp.bfloat16)
+
+
+def reduce_owner(opened, order, after=None):
     trail = []
-    held = parts
-    for axis_name, bit in order:
-        dim = 0 if axis_name == "fsdp" else split_dim(held.shape)
-        own = bit_of(axis_name, bit)
-        other = swap(half_of(held, 1 - own, dim), axis_name, bit)
-        kept = half_of(held, own, dim)
-        held = (kept.astype(jnp.float32) + other.astype(jnp.float32)).astype(jnp.bfloat16)
+    kept, _, other, dim = opened
+    if after is not None:
+        other = tie(other, after)
+    for index, (axis_name, bit) in enumerate(order):
+        if index:
+            kept, _, other, dim = reduce_open(held, order[index:])
+        held = add_low(kept, other)
         if axis_name == "ctx":
             trail.append((bit, dim))
     return held, trail
@@ -318,17 +336,16 @@
     first_bundle = jnp.concatenate(
         [w_query, w_key, w_value, attn_gain[:, None], ffn_gain[:, None]], axis=1
     )
-    first_full = gather_weight(first_bundle)
+    first_full = finish_weight(first_bundle, gather_weight(first_bundle))
     kv_size = KV_HEADS * HEAD
     q_size = HEADS * HEAD
     qkv_size = q_size + 2 * kv_size
     qkv_full = first_full[:, :qkv_size]
     gain_attn = first_full[:, qkv_size]
     gain_ffn = first_full[:, qkv_size + 1]
-    out_full = gather_weight(w_out, first_full)
-    gate_full = gather_weight(w_gate, first_full)
-    up_full = gather_weight(w_up, first_full)
-    down_full = gather_weight(w_down, first_full)
+    out_full = finish_weight(w_out, gather_weight(w_out))
+    later_weights = (w_gate, w_up, w_down)
+    later_pieces = [gather_weight(weight) for weight in later_weights]
     gain_attn = gain_attn.astype(jnp.float32)
     gain_ffn = gain_ffn.astype(jnp.float32)
     slot_ids = jnp.arange(pair_total, dtype=jnp.int32)
@@ -376,6 +393,9 @@
     keys = both_heads[:KV_HEADS]
     values = both_heads[KV_HEADS:]
     mixed_full, lse = attend_forward(queries, keys, values, query_pos, key_pos)
+    gate_full, up_full, down_full = [
+        finish_weight(weight, pieces, lse) for weight, pieces in zip(later_weights, later_pieces)
+    ]
     mixed_low = ungrouped(mixed_full).reshape(local_rows, q_size).astype(jnp.bfloat16)
     residual = inputs + matmul(mixed_low, out_full)
     inverse_two = inverse_rms(residual)
@@ -406,10 +426,8 @@
         return product.reshape((owners, product.shape[0] // owners, product.shape[1]))
 
     down_product = by_owner(hidden, grad_z)
-    down_held, down_trail = reduce_owner(
-        down_product, core_order + fsdp_order + ctx_order
-    )
-    grad_down = spread_owner(down_held, down_trail)[0].astype(jnp.float32)
+    down_kept, _, down_other, down_dim = reduce_open(down_product, core_order)
+    down_open = reduce_open(add_low(down_kept, down_other), fsdp_order + ctx_order)
     gate_up_other = swap(
         by_owner(normed_two, jnp.where(core == 0, grad_up_low, grad_gate_low)), "ctx", 0
     )
@@ -418,22 +436,15 @@
         jnp.bfloat16
     )
     ff_half = gate_up.shape[2] // 2
-    gate_up_sums = []
-    for part_index, part_order in enumerate((fsdp_order + ctx_order, ctx_order + fsdp_order)):
-        columns = gate_up[:, :, part_index * ff_half : (part_index + 1) * ff_half]
-        gate_up_held, gate_up_trail = reduce_owner(columns, part_order)
-        gate_up_sums.append(spread_owner(gate_up_held, gate_up_trail)[0])
-    gate_up_sum = jnp.concatenate(gate_up_sums, axis=1)
-    gate_up_peer = swap(gate_up_sum, "ctx", 0)
-    grad_w_gate = jnp.where(core == 0, gate_up_sum, gate_up_peer).astype(jnp.float32)
-    grad_w_up = jnp.where(core == 0, gate_up_peer, gate_up_sum).astype(jnp.float32)
+    gate_up_orders = (fsdp_order + ctx_order, ctx_order + fsdp_order)
+    gate_up_open = [
+        reduce_open(gate_up[:, :, index * ff_half : (index + 1) * ff_half], order)
+        for index, order in enumerate(gate_up_orders)
+    ]
     grad_resid, grad_ffn_gain_term = norm_back(part, residual, inverse_two, gain_ffn)
     grad_resid = grad_resid + grad_z.astype(jnp.float32)
     grad_attn_low = grad_resid.astype(jnp.bfloat16)
-    out_held, out_trail = reduce_owner(
-        by_owner(mixed_low, grad_attn_low), core_order + fsdp_order + ctx_order
-    )
-    grad_w_out = spread_owner(out_held, out_trail)[0].astype(jnp.float32)
+    out_product = by_owner(mixed_low, grad_attn_low)
     grad_mixed = grouped(contract_cols(grad_attn_low, out_full).astype(jnp.bfloat16))
     grad_queries, grad_keys, grad_values = attend_backward(
         queries,
@@ -444,8 +455,8 @@
         lse,
         mixed_full,
         grad_mixed,
-        gate_up,
-        down_product,
+        gate_up_open[0][1],
+        down_open[1],
     )
     grad_query_rot = ungrouped(grad_queries)
     grad_query_low = (
@@ -462,6 +473,21 @@
         held = kept.astype(jnp.bfloat16) if bit < ctx_bits - 1 else kept
     key_sum = held[0][:, :kv_size]
     value_sum = held[0][:, kv_size:]
+    down_held, down_trail = reduce_owner(down_open, fsdp_order + ctx_order, key_sum)
+    grad_down = spread_owner(down_held, [(0, down_dim)] + down_trail)[0].astype(jnp.float32)
+    gate_up_sums = []
+    for opened, part_order in zip(gate_up_open, gate_up_orders):
+        gate_up_held, gate_up_trail = reduce_owner(opened, part_order, key_sum)
+        gate_up_sums.append(spread_owner(gate_up_held, gate_up_trail)[0])
+    gate_up_sum = jnp.concatenate(gate_up_sums, axis=1)
+    gate_up_peer = swap(gate_up_sum, "ctx", 0)
+    grad_w_gate = jnp.where(core == 0, gate_up_sum, gate_up_peer).astype(jnp.float32)
+    grad_w_up = jnp.where(core == 0, gate_up_peer, gate_up_sum).astype(jnp.float32)
+    full_order = core_order + fsdp_order + ctx_order
+    out_held, out_trail = reduce_owner(
+        reduce_open(tie(out_product, key_sum), full_order), full_order
+    )
+    grad_w_out = spread_owner(out_held, out_trail)[0].astype(jnp.float32)
     grad_key_low = (
         unrotate(key_sum.reshape(local_rows, KV_HEADS, HEAD), cosine_table, sine_table)
         .astype(jnp.bfloat16)
@@ -484,7 +510,7 @@
         ],
         axis=2,
     )
-    qkv_held, qkv_trail = reduce_owner(qkv_parts, core_order + fsdp_order + ctx_order)
+    qkv_held, qkv_trail = reduce_owner(reduce_open(qkv_parts, full_order), full_order)
     qkv_sum = spread_owner(qkv_held, qkv_trail)[0].astype(jnp.float32)
     return (
         block_out,

time: 669 us -> 563 us (0.84)
  waiting for transfers between devices: 254 us -> 157 us
  other arithmetic: 104 us -> 89.1 us
    ppermute x56, waiting for transfers between devices: 186 us -> 128 us  [swap(): lax.ppermute(array, axis_name, [(i, i ^ 1 << bit) for i in range(size)])]
    ppermute x5, waiting for transfers between devices: 68.4 us -> 28.8 us  [gather_weight(): lax.ppermute(part, 'fsdp', [(i, (i + step) % size) for i in range(size)])]
    dynamic_slice x27 -> x25, local copies, waits for them, and re-layouts: 26.7 us -> 22.7 us  [half_of(): return lax.dynamic_slice_in_dim(array, index * size, size, dim)]
    select_n x27 -> x28, other arithmetic: 25.1 us -> 23.1 us  [join(): first = jnp.where(bit == 0, mine, other)]
    unnamed x143 -> x155, local copies, waits for them, and re-layouts: 27.5 us -> 29.3 us
  transfers between devices with their start and end apart: 61 -> 61, of which waited for: 27 -> 32; matrix products, arithmetic and copies ran while one was open for 37% -> 35% of each run, Pallas kernels for 4% -> 2%
where the time goes in v3:
time: 563 us; the launch traced here: 552 us
  waiting for transfers between devices  157 us (28%)
  local copies, waits for them, and re-layouts  149 us (26%)
  other arithmetic  89.1 us (16%)
  starting transfers between devices  87.9 us (16%)
  matrix products  37.8 us (7%)
  Pallas kernels  28.6 us (5%)
    ppermute x56, waiting for transfers between devices, swap(): lax.ppermute(array, axis_name, [(i, i ^ 1 << bit) for i in range(size)])  128 us
    ppermute x56, starting transfers between devices, swap(): lax.ppermute(array, axis_name, [(i, i ^ 1 << bit) for i in range(size)])  82.3 us
    unnamed x155, local copies, waits for them, and re-layouts  29.3 us
    ppermute x5, waiting for transfers between devices, gather_weight(): lax.ppermute(part, 'fsdp', [(i, (i + step) % size) for i in range(size)])  28.8 us
    select_n x28, other arithmetic, join(): first = jnp.where(bit == 0, mine, other)  23.1 us
    dynamic_slice x25, local copies, waits for them, and re-layouts, half_of(): return lax.dynamic_slice_in_dim(array, index * size, size, dim)  22.7 us
    convert_element_type x23, other arithmetic, add_low(): (kept.astype(jnp.float32) + other.astype(jnp.float32)).astype(jnp.bfloat16)  16.5 us
    pallas_call x1, Pallas kernels, attend_backward(): pl.pallas_call(backward_kernel, grid=(heads,), in_specs=[per_head(rows, H...  14.8 us
  transfers between devices with their start and end apart: 61, of which 32 were waited for; matrix products, arithmetic and copies ran while one was open for 35% of the time, Pallas kernels for 2%

profile of v3, /device:TPU:1, one launch (start us, length us, event | category | flops | bytes accessed | tf_op | source)
XLA Modules:
  0.0 552.4 jit_solution(7064969922797519115)
XLA Ops:
  11.4 15.5 %collective-permute-done = bf16[1,240,1602]{2,1,0:T(8,128)(2,1)S(1)} collective-permute-done((bf16[1,240,1602]{2,1,0:T(8,128)(2,1)S(1)}, bf16[1,240,1602]{2,1,0:T(8,128)(2,1)S(1)}, u32[]{:S(2)}, u32[]{:S(2)}) %collective-permute-start) | collective-permute-done | bytes 768992 | tf_op jit(solution)/shard_map/ppermute | solution.py:244
  37.9 7.7 %collective-permute-done.2 = bf16[1,128,640]{1,2,0:T(8,128)(2,1)S(1)} collective-permute-done((bf16[1,128,640]{1,2,0:T(8,128)(2,1)S(1)}, bf16[1,128,640]{1,2,0:T(8,128)(2,1)S(1)}, u32[]{:S(2)}, u32[]{:S(2)}) %collective-permute-start.2) | collective-permute-done | bytes 163872 | tf_op jit(solution)/shard_map/ppermute | solution.py:221
  46.6 7.3 %collective-permute-done.3 = bf16[2,128,640]{1,2,0:T(8,128)(2,1)S(1)} collective-permute-done((bf16[2,128,640]{1,2,0:T(8,128)(2,1)S(1)}, bf16[2,128,640]{1,2,0:T(8,128)(2,1)S(1)}, u32[]{:S(2)}, u32[]{:S(2)}) %collective-permute-start.3) | collective-permute-done | bytes 327712 | tf_op jit(solution)/shard_map/ppermute | solution.py:221
  65.3 5.5 %collective-permute-done.4 = bf16[4,128,640]{2,1,0:T(8,128)(2,1)} collective-permute-done((bf16[4,128,640]{2,1,0:T(8,128)(2,1)S(1)}, bf16[4,128,640]{2,1,0:T(8,128)(2,1)}, u32[]{:S(2)}, u32[]{:S(2)}) %collective-permute-start.4) | collective-permute-done | bytes 655392 | tf_op jit(solution)/shard_map/ppermute | solution.py:221
  82.8 13.3 %collective-permute-done.12 = bf16[1,640,960]{1,2,0:T(8,128)(2,1)} collective-permute-done((bf16[1,640,960]{1,2,0:T(8,128)(2,1)}, bf16[1,640,960]{1,2,0:T(8,128)(2,1)}, u32[]{:S(2)}, u32[]{:S(2)}) %collective-permute-start.12) | collective-permute-done | bytes 1228832 | tf_op jit(solution)/shard_map/ppermute | solution.py:244
  102.4 7.5 %copy.218 = bf16[8,2,128,640]{2,1,0,3:T(2,128)(2,1)} copy(bf16[8,2,128,640]{3,2,0,1:T(8,128)(2,1)} %pad_maximum_fusion.9) | data formatting | bytes 5242880 | tf_op jit(solution)/shard_map/stack | solution.py:389
  109.9 5.5 reshape_reshape.6
  115.3 5.9 %copy.219 = bf16[2048,10,64]{2,0,1:T(8,128)(2,1)} copy(bf16[2048,10,64]{0,2,1:T(8,128)(2,1)} %reshape_reshape.6) | data formatting | bytes 5242880 | tf_op jit(solution)/shard_map/reshape;reshape | solution.py:392
  121.2 5.3 fusion.59
  126.5 13.8 %attend_forward.1 = (f32[5,384,64]{2,1,0:T(8,128)S(1)}, f32[5,384,1]{2,1,0:T(8,128)S(1)}) custom-call(bf16[5,384,64]{2,1,0:T(8,128)(2,1)S(1)} %bitcast.186, bf16[5,2048,64]{2,1,0:T(8,128)(2,1)} %get-tuple-element.98.key_ref, bf16[5,2048,64]{2,1,0:T(8,128)(2,1)} %get-tuple-element.97.value_ref, s32[384,1]{1,0:T(8,128)S(1)} %bitcast.189, ...), custom_call_target="tpu_custom_call" | custom-call | flops 2013265920 | bytes 5242880 | tf_op jit(solution)/shard_map/attend_forward/pallas_call | solution.py:153
  144.2 6.3 %collective-permute-start.13 = (bf16[1,640,960]{1,2,0:T(8,128)(2,1)}, bf16[1,640,960]{1,2,0:T(8,128)(2,1)}, u32[]{:S(2)}, u32[]{:S(2)}) collective-permute-start(bf16[1,640,960]{1,2,0:T(8,128)(2,1)} %copy.224), channel_id=1, source_target_pairs={{0,2},{2,0},{4,6},{6,4},{8,10},{10,8},{12,14},{14,12},{16,18},{18,... | collective-permute-start | bytes 3686408 | tf_op jit(solution)/shard_map/ppermute | solution.py:221
  184.7 7.9 %copy.231 = bf16[2560,960]{1,0:T(8,128)(2,1)} copy(bf16[2560,960]{0,1:T(8,128)(2,1)} %convolution_convert_fusion) | data formatting | bytes 9830400 | tf_op jit(solution)/shard_map/convert_element_type | solution.py:425
  231.1 14.8 %attend_backward.1 = (f32[5,384,64]{2,1,0:T(8,128)S(1)}, bf16[5,2048,64]{2,1,0:T(8,128)(2,1)}, bf16[5,2048,64]{2,1,0:T(8,128)(2,1)}) custom-call(bf16[5,384,64]{2,1,0:T(8,128)(2,1)S(1)} %bitcast.187, bf16[5,2048,64]{2,1,0:T(8,128)(2,1)} %get-tuple-element.98.key_ref, bf16[5,2048,64]{2,1,0:T(8,128)(2,1)} %get-tuple-element.97.value_ref, ...), custom_call_target="tpu_custom_call" | custom-call | flops 10066329600 | bytes 10485760 | tf_op jit(solution)/shard_map/attend_backward/pallas_call | solution.py:184
  245.9 5.9 %maximum_bitcast_fusion = bf16[2048,10,64]{2,0,1:T(8,128)(2,1)} fusion(bf16[5,2048,64]{2,1,0:T(8,128)(2,1)} %get-tuple-element.20, bf16[5,2048,64]{2,1,0:T(8,128)(2,1)} %get-tuple-element.19), kind=kLoop, calls=%fused_computation.6 | loop fusion | flops 1310720 | bytes 5242880 | tf_op jit(solution)/shard_map/transpose | solution.py:467
  251.8 6.1 %copy.236 = bf16[2048,10,64]{0,2,1:T(8,128)(2,1)} copy(bf16[2048,10,64]{2,0,1:T(8,128)(2,1)} %maximum_bitcast_fusion) | data formatting | bytes 5242880 | tf_op jit(solution)/shard_map/transpose | solution.py:467
  257.9 5.6 %reshape_reshape.7 = bf16[8,2,128,640]{2,1,0,3:T(2,128)(2,1)} reshape(bf16[2048,10,64]{0,2,1:T(8,128)(2,1)} %copy.236) | data formatting | bytes 5242880 | tf_op jit(solution)/shard_map/reshape;reshape | solution.py:471
  263.4 6.9 %fusion.62 = (bf16[8,1,128,640]{2,1,0,3:T(2,128)(2,1)S(1)}, f32[8,1,128,640]{2,1,0,3:T(1,128)S(1)}) fusion(bf16[8,2,128,640]{2,1,0,3:T(2,128)(2,1)} %reshape_reshape.7), kind=kLoop, calls=%fused_computation.275 | loop fusion | flops 655360 | bytes 6553600 | tf_op jit(solution)/shard_map/slice | solution.py:472
  284.3 5.1 fusion.17
  291.1 5.9 %collective-permute-done.17 = bf16[4,128,640]{2,1,0:T(8,128)(2,1)} collective-permute-done((bf16[4,128,640]{2,1,0:T(8,128)(2,1)}, bf16[4,128,640]{2,1,0:T(8,128)(2,1)}, u32[]{:S(2)}, u32[]{:S(2)}) %collective-permute-start.17) | collective-permute-done | bytes 655392 | tf_op jit(solution)/shard_map/ppermute | solution.py:221
  303.3 8.5 %collective-permute-done.53 = bf16[1,640,960]{1,2,0:T(8,128)(2,1)} collective-permute-done((bf16[1,640,960]{1,2,0:T(8,128)(2,1)}, bf16[1,640,960]{1,2,0:T(8,128)(2,1)}, u32[]{:S(2)}, u32[]{:S(2)}) %collective-permute-start.53) | collective-permute-done | bytes 1228832 | tf_op jit(solution)/shard_map/ppermute | solution.py:221
  323.8 4.8 collective-permute-done.19
  335.9 6.0 %concatenate.143 = bf16[2,480,1792]{2,1,0:T(8,128)(2,1)} concatenate(bf16[2,480,1600]{2,1,0:T(8,128)(2,1)S(1)} %bitcast.194, bf16[2,480,1]{2,1,0:T(8,128)(2,1)S(1)} %stack.62, bf16[2,480,1]{2,1,0:T(8,128)(2,1)} %stack.63, bf16[2,480,190]{2,1,0:T(8,128)(2,1)} %broadcast_in_dim.79), dimensions={2} | concatenate | bytes 6881280 | tf_op jit(solution)/shard_map/concatenate | solution.py:505
  372.6 11.3 %collective-permute-done.54 = bf16[1,320,960]{2,1,0:T(8,128)(2,1)S(1)} collective-permute-done((bf16[1,320,960]{2,1,0:T(8,128)(2,1)S(1)}, bf16[1,320,960]{2,1,0:T(8,128)(2,1)S(1)}, u32[]{:S(2)}, u32[]{:S(2)}) %collective-permute-start.54) | collective-permute-done | bytes 614432 | tf_op jit(solution)/shard_map/ppermute | solution.py:221
  399.3 6.1 %collective-permute-start.49 = (bf16[1,120,640]{2,1,0:T(8,128)(2,1)S(1)}, bf16[1,120,640]{2,1,0:T(8,128)(2,1)S(1)}, u32[]{:S(2)}, u32[]{:S(2)}) collective-permute-start(bf16[1,120,640]{2,1,0:T(8,128)(2,1)S(1)} %add_convert_fusion.19), channel_id=1, source_target_pairs={{0,16},{2,18},{4,20},{6,22},{8,24},{10,26},{12,28},{14,30},{16,0},... | collective-permute-start | bytes 460808 | tf_op jit(solution)/shard_map/ppermute | solution.py:221
  408.0 10.0 %collective-permute-done.49 = bf16[1,120,640]{2,1,0:T(8,128)(2,1)S(1)} collective-permute-done((bf16[1,120,640]{2,1,0:T(8,128)(2,1)S(1)}, bf16[1,120,640]{2,1,0:T(8,128)(2,1)S(1)}, u32[]{:S(2)}, u32[]{:S(2)}) %collective-permute-start.49) | collective-permute-done | bytes 153632 | tf_op jit(solution)/shard_map/ppermute | solution.py:221
  421.5 5.0 collective-permute-done.57
  463.9 7.3 %collective-permute-done.59 = bf16[1,320,960]{2,1,0:T(8,128)(2,1)S(1)} collective-permute-done((bf16[1,320,960]{2,1,0:T(8,128)(2,1)S(1)}, bf16[1,320,960]{2,1,0:T(8,128)(2,1)S(1)}, u32[]{:S(2)}, u32[]{:S(2)}) %collective-permute-start.59) | collective-permute-done | bytes 614432 | tf_op jit(solution)/shard_map/ppermute | solution.py:221
  476.1 7.4 %collective-permute-start.60 = (bf16[1,640,960]{1,2,0:T(8,128)(2,1)}, bf16[1,640,960]{1,2,0:T(8,128)(2,1)}, u32[]{:S(2)}, u32[]{:S(2)}) collective-permute-start(bf16[1,640,960]{1,2,0:T(8,128)(2,1)} %copy.249), channel_id=1, source_target_pairs={{0,2},{2,0},{4,6},{6,4},{8,10},{10,8},{12,14},{14,12},{16,18},{18,... | collective-permute-start | bytes 3686408 | tf_op jit(solution)/shard_map/ppermute | solution.py:221
  490.6 8.6 %collective-permute-done.22 = bf16[1,120,1792]{2,1,0:T(8,128)(2,1)S(1)} collective-permute-done((bf16[1,120,1792]{2,1,0:T(8,128)(2,1)S(1)}, bf16[1,120,1792]{2,1,0:T(8,128)(2,1)S(1)}, u32[]{:S(2)}, u32[]{:S(2)}) %collective-permute-start.22) | collective-permute-done | bytes 430112 | tf_op jit(solution)/shard_map/ppermute | solution.py:221
  528.8 5.8 %copy.254 = f32[1280,960]{0,1:T(8,128)} copy(f32[1280,960]{1,0:T(8,128)} %fusion.6) | data formatting | bytes 9830400
  534.8 4.8 collective-permute-start.28
  539.6 6.9 %select_convert_fusion = (f32[480,2560]{1,0:T(8,128)}, f32[480,2560]{1,0:T(8,128)}) fusion(bf16[480,2560]{1,0:T(8,128)(2,1)} %collective-permute-done.52, pred[]{:T(512)S(6)} %eq.21, bf16[480,1280]{1,0:T(8,128)(2,1)S(1)} %maximum_bitcast_fusion.8, bf16[480,1280]{1,0:T(8,128)(2,1)S(1)} %maximum_bitcast_fusion.7), kind=kLoop, calls=%fused_computation.31 | loop fusion | flops 9830400 | bytes 14745601 | tf_op jit(solution)/shard_map/convert_element_type | solution.py:485
  (458 shorter events, 305.1 us)
Async XLA Ops:
  7.3 19.6 %collective-permute-start = (bf16[1,240,1602]{2,1,0:T(8,128)(2,1)S(1)}, bf16[1,240,1602]{2,1,0:T(8,128)(2,1)S(1)}, u32[]{:S(2)}, u32[]{:S(2)}) collective-permute-start(bf16[1,240,1602]{2,1,0:T(8,128)(2,1)S(1)} %dynamic-slice_bitcast_fusion.3), channel_id=1, source_target_pairs={{0,1},{1,0},{2,3},{3,2},{4,5},{5,4},{6,7},{7,6},{8,9},{9,8},{10,11... | collective-permute-start | bytes 2306888 | tf_op jit(solution)/shard_map/ppermute | solution.py:244
  59.1 23.3 %collective-permute-start.6 = (bf16[1,240,960]{2,1,0:T(8,128)(2,1)}, bf16[1,240,960]{2,1,0:T(8,128)(2,1)}, u32[]{:S(2)}, u32[]{:S(2)}) collective-permute-start(bf16[1,240,960]{2,1,0:T(8,128)(2,1)} %dynamic-slice_bitcast_fusion.4), channel_id=1, source_target_pairs={{0,1},{1,0},{2,3},{3,2},{4,5},{5,4},{6,7},{7,6},{8,9},{9,8},{10,11... | collective-permute-start | bytes 1382408 | tf_op jit(solution)/shard_map/ppermute | solution.py:244
  62.7 33.3 %collective-permute-start.12 = (bf16[1,640,960]{1,2,0:T(8,128)(2,1)}, bf16[1,640,960]{1,2,0:T(8,128)(2,1)}, u32[]{:S(2)}, u32[]{:S(2)}) collective-permute-start(bf16[1,640,960]{1,2,0:T(8,128)(2,1)} %dynamic-slice_bitcast_fusion), channel_id=1, source_target_pairs={{0,1},{1,0},{2,3},{3,2},{4,5},{5,4},{6,7},{7,6},{8,9},{9,8},{10,11... | collective-permute-start | bytes 3686408 | tf_op jit(solution)/shard_map/ppermute | solution.py:244
  64.1 86.4 %collective-permute-start.10 = (bf16[1,240,2560]{2,1,0:T(8,128)(2,1)}, bf16[1,240,2560]{2,1,0:T(8,128)(2,1)}, u32[]{:S(2)}, u32[]{:S(2)}) collective-permute-start(bf16[1,240,2560]{2,1,0:T(8,128)(2,1)} %dynamic-slice_bitcast_fusion.1), channel_id=1, source_target_pairs={{0,1},{1,0},{2,3},{3,2},{4,5},{5,4},{6,7},{7,6},{8,9},{9,8},{10,11... | collective-permute-start | bytes 3686408 | tf_op jit(solution)/shard_map/ppermute | solution.py:244
  73.4 25.5 %collective-permute-start.5 = (bf16[8,128,640]{2,1,0:T(8,128)(2,1)}, bf16[8,128,640]{2,1,0:T(8,128)(2,1)}, u32[]{:S(2)}, u32[]{:S(2)}) collective-permute-start(bf16[8,128,640]{2,1,0:T(8,128)(2,1)} %bitcast.22), channel_id=1, source_target_pairs={{0,2},{2,0},{4,6},{6,4},{8,10},{10,8},{12,14},{14,12},{16,18},{18,... | collective-permute-start | bytes 3932168 | tf_op jit(solution)/shard_map/ppermute | solution.py:221
  77.4 77.7 %collective-permute-start.8 = (bf16[1,240,2560]{2,1,0:T(8,128)(2,1)}, bf16[1,240,2560]{2,1,0:T(8,128)(2,1)}, u32[]{:S(2)}, u32[]{:S(2)}) collective-permute-start(bf16[1,240,2560]{2,1,0:T(8,128)(2,1)} %dynamic-slice_bitcast_fusion.2), channel_id=1, source_target_pairs={{0,1},{1,0},{2,3},{3,2},{4,5},{5,4},{6,7},{7,6},{8,9},{9,8},{10,11... | collective-permute-start | bytes 3686408 | tf_op jit(solution)/shard_map/ppermute | solution.py:244
  82.4 68.2 %collective-permute-start.7 = (bf16[1,240,960]{2,1,0:T(8,128)(2,1)}, bf16[1,240,960]{2,1,0:T(8,128)(2,1)S(1)}, u32[]{:S(2)}, u32[]{:S(2)}) collective-permute-start(bf16[1,240,960]{2,1,0:T(8,128)(2,1)} %collective-permute-done.6), channel_id=1, source_target_pairs={{0,2},{2,0},{4,6},{6,4},{8,10},{10,8},{12,14},{14,12},{16,18},{18,... | collective-permute-start | bytes 1382408 | tf_op jit(solution)/shard_map/ppermute | solution.py:221
  180.9 42.2 %collective-permute-start.14 = (bf16[2,480,2560]{2,1,0:T(8,128)(2,1)}, bf16[2,480,2560]{2,1,0:T(8,128)(2,1)}, u32[]{:S(2)}, u32[]{:S(2)}) collective-permute-start(bf16[2,480,2560]{2,1,0:T(8,128)(2,1)} %bitcast.44), channel_id=1, source_target_pairs={{0,2},{2,0},{4,6},{6,4},{8,10},{10,8},{12,14},{14,12},{16,18},{18,... | collective-permute-start | bytes 14745608 | tf_op jit(solution)/shard_map/ppermute | solution.py:221
  280.5 16.5 %collective-permute-start.17 = (bf16[4,128,640]{2,1,0:T(8,128)(2,1)}, bf16[4,128,640]{2,1,0:T(8,128)(2,1)}, u32[]{:S(2)}, u32[]{:S(2)}) collective-permute-start(bf16[4,128,640]{2,1,0:T(8,128)(2,1)} %bitcast.215), channel_id=1, source_target_pairs={{0,4},{2,6},{4,0},{6,2},{8,12},{10,14},{12,8},{14,10},{16,20},{18,... | collective-permute-start | bytes 1966088 | tf_op jit(solution)/shard_map/ppermute | solution.py:221
  283.3 28.5 %collective-permute-start.53 = (bf16[1,640,960]{1,2,0:T(8,128)(2,1)}, bf16[1,640,960]{1,2,0:T(8,128)(2,1)}, u32[]{:S(2)}, u32[]{:S(2)}) collective-permute-start(bf16[1,640,960]{1,2,0:T(8,128)(2,1)} %copy.247), channel_id=1, source_target_pairs={{0,1},{1,0},{2,3},{3,2},{4,5},{5,4},{6,7},{7,6},{8,9},{9,8},{10,11... | collective-permute-start | bytes 3686408 | tf_op jit(solution)/shard_map/ppermute | solution.py:221
  299.1 18.4 %collective-permute-start.18 = (bf16[2,128,640]{2,1,0:T(8,128)(2,1)}, bf16[2,128,640]{2,1,0:T(8,128)(2,1)}, u32[]{:S(2)}, u32[]{:S(2)}) collective-permute-start(bf16[2,128,640]{2,1,0:T(8,128)(2,1)} %slice_bitcast_fusion), channel_id=1, source_target_pairs={{0,8},{2,10},{4,12},{6,14},{8,0},{10,2},{12,4},{14,6},{16,24},{18,... | collective-permute-start | bytes 983048 | tf_op jit(solution)/shard_map/ppermute | solution.py:221
  314.2 39.6 %collective-permute-start.38 = (bf16[1,480,1280]{2,1,0:T(8,128)(2,1)}, bf16[1,480,1280]{2,1,0:T(8,128)(2,1)}, u32[]{:S(2)}, u32[]{:S(2)}) collective-permute-start(bf16[1,480,1280]{2,1,0:T(8,128)(2,1)} %constant_dynamic-slice_fusion.22.after_ref), channel_id=1, source_target_pairs={{0,1},{1,0},{2,3},{3,2},{4,5},{5,4},{6,7},{7,6},{8,9},{9,8},{10,11... | collective-permute-start | bytes 3686408 | tf_op jit(solution)/shard_map/ppermute | solution.py:221
  321.8 27.1 %collective-permute-start.45 = (bf16[2,240,1280]{2,1,0:T(8,128)(2,1)}, bf16[2,240,1280]{2,1,0:T(8,128)(2,1)}, u32[]{:S(2)}, u32[]{:S(2)}) collective-permute-start(bf16[2,240,1280]{2,1,0:T(8,128)(2,1)} %constant_dynamic-slice_fusion.6), channel_id=1, source_target_pairs={{0,4},{2,6},{4,0},{6,2},{8,12},{10,14},{12,8},{14,10},{16,20},{18,... | collective-permute-start | bytes 3686408 | tf_op jit(solution)/shard_map/ppermute | solution.py:221
  344.7 108.0 %collective-permute-start.20 = (bf16[2,240,1792]{2,1,0:T(8,128)(2,1)}, bf16[2,240,1792]{2,1,0:T(8,128)(2,1)}, u32[]{:S(2)}, u32[]{:S(2)}) collective-permute-start(bf16[2,240,1792]{2,1,0:T(8,128)(2,1)} %constant_dynamic-slice_fusion.19), channel_id=1, source_target_pairs={{0,2},{2,0},{4,6},{6,4},{8,10},{10,8},{12,14},{14,12},{16,18},{18,... | collective-permute-start | bytes 5160968 | tf_op jit(solution)/shard_map/ppermute | solution.py:221
  348.8 36.8 %collective-permute-start.29 = (bf16[2,240,960]{2,1,0:T(8,128)(2,1)}, bf16[2,240,960]{2,1,0:T(8,128)(2,1)}, u32[]{:S(2)}, u32[]{:S(2)}) collective-permute-start(bf16[2,240,960]{2,1,0:T(8,128)(2,1)} %constant_dynamic-slice_fusion.14), channel_id=1, source_target_pairs={{0,2},{2,0},{4,6},{6,4},{8,10},{10,8},{12,14},{14,12},{16,18},{18,... | collective-permute-start | bytes 2764808 | tf_op jit(solution)/shard_map/ppermute | solution.py:221
  360.6 23.3 %collective-permute-start.54 = (bf16[1,320,960]{2,1,0:T(8,128)(2,1)S(1)}, bf16[1,320,960]{2,1,0:T(8,128)(2,1)S(1)}, u32[]{:S(2)}, u32[]{:S(2)}) collective-permute-start(bf16[1,320,960]{2,1,0:T(8,128)(2,1)S(1)} %constant_dynamic-slice_fusion.2), channel_id=1, source_target_pairs={{0,4},{2,6},{4,0},{6,2},{8,12},{10,14},{12,8},{14,10},{16,20},{18,... | collective-permute-start | bytes 1843208 | tf_op jit(solution)/shard_map/ppermute | solution.py:221
  365.5 22.0 %collective-permute-start.47 = (bf16[2,120,640]{2,1,0:T(8,128)(2,1)S(1)}, bf16[2,120,640]{2,1,0:T(8,128)(2,1)S(1)}, u32[]{:S(2)}, u32[]{:S(2)}) collective-permute-start(bf16[2,120,640]{2,1,0:T(8,128)(2,1)S(1)} %constant_dynamic-slice_fusion.4), channel_id=1, source_target_pairs={{0,16},{2,18},{4,20},{6,22},{8,24},{10,26},{12,28},{14,30},{16,0},... | collective-permute-start | bytes 921608 | tf_op jit(solution)/shard_map/ppermute | solution.py:221
  371.2 17.7 %collective-permute-start.40 = (bf16[1,120,1280]{2,1,0:T(8,128)(2,1)S(1)}, bf16[1,120,1280]{2,1,0:T(8,128)(2,1)S(1)}, u32[]{:S(2)}, u32[]{:S(2)}) collective-permute-start(bf16[1,120,1280]{2,1,0:T(8,128)(2,1)S(1)} %constant_dynamic-slice_fusion.8), channel_id=1, source_target_pairs={{0,8},{2,10},{4,12},{6,14},{8,0},{10,2},{12,4},{14,6},{16,24},{18,... | collective-permute-start | bytes 921608 | tf_op jit(solution)/shard_map/ppermute | solution.py:221
  387.2 39.5 %collective-permute-start.30 = (bf16[1,240,960]{2,1,0:T(8,128)(2,1)S(1)}, bf16[1,240,960]{2,1,0:T(8,128)(2,1)S(1)}, u32[]{:S(2)}, u32[]{:S(2)}) collective-permute-start(bf16[1,240,960]{2,1,0:T(8,128)(2,1)S(1)} %constant_dynamic-slice_fusion.13), channel_id=1, source_target_pairs={{0,1},{1,0},{2,3},{3,2},{4,5},{5,4},{6,7},{7,6},{8,9},{9,8},{10,11... | collective-permute-start | bytes 1382408 | tf_op jit(solution)/shard_map/ppermute | solution.py:221
  389.0 16.4 %collective-permute-start.41 = (bf16[1,120,640]{2,1,0:T(8,128)(2,1)S(1)}, bf16[1,120,640]{2,1,0:T(8,128)(2,1)S(1)}, u32[]{:S(2)}, u32[]{:S(2)}) collective-permute-start(bf16[1,120,640]{2,1,0:T(8,128)(2,1)S(1)} %constant_dynamic-slice_fusion.7), channel_id=1, source_target_pairs={{0,16},{2,18},{4,20},{6,22},{8,24},{10,26},{12,28},{14,30},{16,0},... | collective-permute-start | bytes 460808 | tf_op jit(solution)/shard_map/ppermute | solution.py:221
  399.3 18.6 %collective-permute-start.49 = (bf16[1,120,640]{2,1,0:T(8,128)(2,1)S(1)}, bf16[1,120,640]{2,1,0:T(8,128)(2,1)S(1)}, u32[]{:S(2)}, u32[]{:S(2)}) collective-permute-start(bf16[1,120,640]{2,1,0:T(8,128)(2,1)S(1)} %add_convert_fusion.19), channel_id=1, source_target_pairs={{0,16},{2,18},{4,20},{6,22},{8,24},{10,26},{12,28},{14,30},{16,0},... | collective-permute-start | bytes 460808 | tf_op jit(solution)/shard_map/ppermute | solution.py:221
  406.0 20.5 %collective-permute-start.57 = (bf16[1,80,960]{2,1,0:T(8,128)(2,1)S(1)}, bf16[1,80,960]{2,1,0:T(8,128)(2,1)S(1)}, u32[]{:S(2)}, u32[]{:S(2)}) collective-permute-start(bf16[1,80,960]{2,1,0:T(8,128)(2,1)S(1)} %add_convert_fusion.18), channel_id=1, source_target_pairs={{0,16},{2,18},{4,20},{6,22},{8,24},{10,26},{12,28},{14,30},{16,0},... | collective-permute-start | bytes 460808 | tf_op jit(solution)/shard_map/ppermute | solution.py:221
  421.3 16.4 %collective-permute-start.43 = (bf16[1,120,1280]{2,1,0:T(8,128)(2,1)S(1)}, bf16[1,120,1280]{2,1,0:T(8,128)(2,1)S(1)}, u32[]{:S(2)}, u32[]{:S(2)}) collective-permute-start(bf16[1,120,1280]{2,1,0:T(8,128)(2,1)S(1)} %pad_maximum_fusion.38), channel_id=1, source_target_pairs={{0,8},{2,10},{4,12},{6,14},{8,0},{10,2},{12,4},{14,6},{16,24},{18,... | collective-permute-start | bytes 921608 | tf_op jit(solution)/shard_map/ppermute | solution.py:221
  426.6 18.3 %collective-permute-start.58 = (bf16[1,160,960]{2,1,0:T(8,128)(2,1)S(1)}, bf16[1,160,960]{2,1,0:T(8,128)(2,1)S(1)}, u32[]{:S(2)}, u32[]{:S(2)}) collective-permute-start(bf16[1,160,960]{2,1,0:T(8,128)(2,1)S(1)} %pad_maximum_fusion.37), channel_id=1, source_target_pairs={{0,8},{2,10},{4,12},{6,14},{8,0},{10,2},{12,4},{14,6},{16,24},{18,... | collective-permute-start | bytes 921608 | tf_op jit(solution)/shard_map/ppermute | solution.py:221
  432.1 51.4 %collective-permute-start.51 = (bf16[1,240,1280]{2,1,0:T(8,128)(2,1)}, bf16[1,240,1280]{2,1,0:T(8,128)(2,1)}, u32[]{:S(2)}, u32[]{:S(2)}) collective-permute-start(bf16[1,240,1280]{2,1,0:T(8,128)(2,1)} %pad_maximum_fusion.32), channel_id=1, source_target_pairs={{0,4},{2,6},{4,0},{6,2},{8,12},{10,14},{12,8},{14,10},{16,20},{18,... | collective-permute-start | bytes 1843208 | tf_op jit(solution)/shard_map/ppermute | solution.py:221
  438.7 46.2 %collective-permute-start.44 = (bf16[1,240,1280]{2,1,0:T(8,128)(2,1)}, bf16[1,240,1280]{2,1,0:T(8,128)(2,1)}, u32[]{:S(2)}, u32[]{:S(2)}) collective-permute-start(bf16[1,240,1280]{2,1,0:T(8,128)(2,1)} %pad_maximum_fusion.31), channel_id=1, source_target_pairs={{0,4},{2,6},{4,0},{6,2},{8,12},{10,14},{12,8},{14,10},{16,20},{18,... | collective-permute-start | bytes 1843208 | tf_op jit(solution)/shard_map/ppermute | solution.py:221
  448.3 22.9 %collective-permute-start.59 = (bf16[1,320,960]{2,1,0:T(8,128)(2,1)S(1)}, bf16[1,320,960]{2,1,0:T(8,128)(2,1)S(1)}, u32[]{:S(2)}, u32[]{:S(2)}) collective-permute-start(bf16[1,320,960]{2,1,0:T(8,128)(2,1)S(1)} %pad_maximum_fusion.30), channel_id=1, source_target_pairs={{0,4},{2,6},{4,0},{6,2},{8,12},{10,14},{12,8},{14,10},{16,20},{18,... | collective-permute-start | bytes 1843208 | tf_op jit(solution)/shard_map/ppermute | solution.py:221
  457.9 28.3 %collective-permute-start.21 = (bf16[1,240,1792]{2,1,0:T(8,128)(2,1)}, bf16[1,240,1792]{2,1,0:T(8,128)(2,1)}, u32[]{:S(2)}, u32[]{:S(2)}) collective-permute-start(bf16[1,240,1792]{2,1,0:T(8,128)(2,1)} %constant_dynamic-slice_fusion.18), channel_id=1, source_target_pairs={{0,1},{1,0},{2,3},{3,2},{4,5},{5,4},{6,7},{7,6},{8,9},{9,8},{10,11... | collective-permute-start | bytes 2580488 | tf_op jit(solution)/shard_map/ppermute | solution.py:221
  462.6 26.4 %collective-permute-start.36 = (bf16[1,120,960]{2,1,0:T(8,128)(2,1)}, bf16[1,120,960]{2,1,0:T(8,128)(2,1)}, u32[]{:S(2)}, u32[]{:S(2)}) collective-permute-start(bf16[1,120,960]{2,1,0:T(8,128)(2,1)} %pad_maximum_fusion.42), channel_id=1, source_target_pairs={{0,4},{2,6},{4,0},{6,2},{8,12},{10,14},{12,8},{14,10},{16,20},{18,... | collective-permute-start | bytes 691208 | tf_op jit(solution)/shard_map/ppermute | solution.py:221
  476.1 38.3 %collective-permute-start.60 = (bf16[1,640,960]{1,2,0:T(8,128)(2,1)}, bf16[1,640,960]{1,2,0:T(8,128)(2,1)}, u32[]{:S(2)}, u32[]{:S(2)}) collective-permute-start(bf16[1,640,960]{1,2,0:T(8,128)(2,1)} %copy.249), channel_id=1, source_target_pairs={{0,2},{2,0},{4,6},{6,4},{8,10},{10,8},{12,14},{14,12},{16,18},{18,... | collective-permute-start | bytes 3686408 | tf_op jit(solution)/shard_map/ppermute | solution.py:221
  490.2 17.8 %collective-permute-start.37 = (bf16[1,240,960]{2,1,0:T(8,128)(2,1)S(1)}, bf16[1,240,960]{2,1,0:T(8,128)(2,1)S(1)}, u32[]{:S(2)}, u32[]{:S(2)}) collective-permute-start(bf16[1,240,960]{2,1,0:T(8,128)(2,1)S(1)} %pad_maximum_fusion.33), channel_id=1, source_target_pairs={{0,2},{2,0},{4,6},{6,4},{8,10},{10,8},{12,14},{14,12},{16,18},{18,... | collective-permute-start | bytes 1382408 | tf_op jit(solution)/shard_map/ppermute | solution.py:221
  502.2 37.4 %collective-permute-start.52 = (bf16[480,2560]{1,0:T(8,128)(2,1)}, bf16[480,2560]{1,0:T(8,128)(2,1)}, u32[]{:S(2)}, u32[]{:S(2)}) collective-permute-start(bf16[480,2560]{1,0:T(8,128)(2,1)} %pad_maximum_fusion.10), channel_id=1, source_target_pairs={{0,2},{2,0},{4,6},{6,4},{8,10},{10,8},{12,14},{14,12},{16,18},{18,... | collective-permute-start | bytes 7372808 | tf_op jit(solution)/shard_map/ppermute | solution.py:221
  (102 other events, 1354.0 us)
